TPU v7x, 128 devices: a whole 4x4x4 slice. The times are simulated.
128 devices in a mesh: ctx: 8 (over x_hi, y), fsdp: 16 (over x_lo, z, core).
Axes of the slice: x: 4 (x_hi: 2, x_lo: 2; x = x_hi * 2 + x_lo), y: 4, z: 4, core: 2. Of those that a mesh axis runs over, the one named last changes fastest.
Arguments:
- tokens: bfloat16 [16, 1024, 1024], P('fsdp', 'ctx'), may hold values from -6 to 6
- d_out: bfloat16 [16, 1024, 1024], P('fsdp', 'ctx'), may hold values from -6 to 6
- block_ids: int32 [16, 16], P('fsdp'), may hold values from 0 to 15, as said below
- w_qkv: float32 [1024, 4096], P('fsdp'), may hold values from -0.1875 to 0.1875
- w_out: float32 [2048, 1024], P('fsdp'), may hold values from -2 to 2
- w_gate_up: float32 [1024, 6144], P('fsdp'), may hold values from -0.1875 to 0.1875
- w_down: float32 [3072, 1024], P('fsdp'), may hold values from -0.21875 to 0.21875
- gains: float32 [2304], P('fsdp'), may hold values from 0.5 to 1.5
- moment_qkv: float32 [1024, 4096], P('fsdp'), may hold values from -64 to 64
- moment_out: float32 [2048, 1024], P('fsdp'), may hold values from -7 to 7
- moment_gate_up: float32 [1024, 6144], P('fsdp'), may hold values from -56 to 56
- moment_down: float32 [3072, 1024], P('fsdp'), may hold values from -48 to 48
- moment_gains: float32 [2304], P('fsdp'), may hold values from -128 to 128
- square_qkv: float32 [1024, 4096], P('fsdp'), may hold values from 245.76 to 3276.8
- square_out: float32 [2048, 1024], P('fsdp'), may hold values from 3.2 to 44.8
- square_gate_up: float32 [1024, 6144], P('fsdp'), may hold values from 212.992 to 2785.28
- square_down: float32 [3072, 1024], P('fsdp'), may hold values from 180.224 to 2293.76
- square_gains: float32 [2304], P('fsdp'), may hold values from 1146.88 to 14745.6
Outputs:
- out_tokens: bfloat16 [16, 1024, 1024], P('fsdp', 'ctx')
- d_tokens: bfloat16 [16, 1024, 1024], P('fsdp', 'ctx')
- updated_qkv: float32 [1024, 4096], P('fsdp')
- updated_out: float32 [2048, 1024], P('fsdp')
- updated_gate_up: float32 [1024, 6144], P('fsdp')
- updated_down: float32 [3072, 1024], P('fsdp')
- updated_gains: float32 [2304], P('fsdp')
- next_moment_qkv: float32 [1024, 4096], P('fsdp')
- next_moment_out: float32 [2048, 1024], P('fsdp')
- next_moment_gate_up: float32 [1024, 6144], P('fsdp')
- next_moment_down: float32 [3072, 1024], P('fsdp')
- next_moment_gains: float32 [2304], P('fsdp')
- next_square_qkv: float32 [1024, 4096], P('fsdp')
- next_square_out: float32 [2048, 1024], P('fsdp')
- next_square_gate_up: float32 [1024, 6144], P('fsdp')
- next_square_down: float32 [3072, 1024], P('fsdp')
- next_square_gains: float32 [2304], P('fsdp')
Inputs may be any that keep to these rules, and one draw needn't show every extreme that they name: `block_ids`: in each sequence, the two stored blocks of index 2 r and 2 r + 1 are the blocks c and 15 - c for some c, in either order; every block of a sequence is stored once.
All inputs are finite; a program needn't handle non-finite values.
Results may differ from a plain program's by a relative error of at most 0.033.
Values may be sent and summed in bfloat16 or wider, within the bound.
A program may use at most 192 MiB of HBM per device.

v0:
```python
import math
import types

import jax
import jax.numpy as jnp
import numpy as np
from jax import lax
from jax.experimental import pallas as pl
from jax.experimental.pallas import tpu as pltpu
from jax.sharding import PartitionSpec as P

D = 1024
HEAD = 128
STEP = 10
BLOCK = 64
norm_eps = 1e-06
rope_base = 1000000.0
beta_first = 0.9
beta_second = 0.95
adam_eps = 1e-08
decay_rate = 0.1
SCALE = 1.0 / math.sqrt(HEAD)

f32 = jnp.float32
bf16 = jnp.bfloat16
MESH = pl.DeviceIdType.MESH

INPUTS = dict(
    tok=False, dyt=False, pos_in=False, gain_in=False, freq=False, wqkv_f=True, wo_f=False, wgu_f=True, wd_f=False
)
OUTPUTS = dict(
    out_tok=((128, D), bf16),
    dtok=((128, D), bf16),
    g_qkv=((64, 4096), bf16),
    g_out=((128, D), bf16),
    g_gu=((64, 6144), bf16),
    g_dn=((192, D), bf16),
    g_gain=((24, 128), f32),
)
BUFFERS = dict(
    x_all=((4, 2, 128, D), bf16),
    dy_all=((4, 2, 128, D), bf16),
    n2_all=((4, 2, 128, D), bf16),
    n1_all=((4, 256, D), bf16),
    wq_f=((2, 64, 512), f32),
    wgu_fs=((2, 64, 768), f32),
    wq_send=((2, 64, 512), bf16),
    wgu_send=((2, 64, 768), bf16),
    wo_own=((128, D), bf16),
    wd_own=((192, D), bf16),
    wq=((16, 64, 512), bf16),
    wgu=((16, 64, 768), bf16),
    wo=((256, D), bf16),
    wd=((384, D), bf16),
    gain_recv=((16, 24, 128), f32),
    pos=((2, 8, D), f32),
    posk=((2, D, 1), f32),
    cos_t=((4, 256, HEAD), f32),
    sin_t=((4, 256, HEAD), f32),
    qkraw=((4, 256, 384), f32),
    q_s=((2, 2, 256, 256), bf16),
    kv=((2, D, 256), bf16),
    o_t=((2, 256, 512), f32),
    ob_t=((2, 256, 512), bf16),
    lse=((2, 2, 1, 512), f32),
    pa=((4, 2, 128, D), bf16),
    pb=((4, 2, 128, D), bf16),
    ca=((4, 128, D), bf16),
    cb=((4, 128, D), bf16),
    ra=((3, 128, D), bf16),
    rb=((3, 128, D), bf16),
    h1=((128, D), f32),
    dh1=((128, D), f32),
    hid_all=((4, 2, 128, 384), bf16),
    dgu_all=((4, 2, 128, 768), bf16),
    do_t=((2, 256, 512), bf16),
    delta=((2, 2, 1, 512), f32),
    dkv=((2, D, 256), f32),
    dkv_send=((2, 512, 256), bf16),
    dkv_recv=((2, 512, 256), bf16),
    dqkv=((4, 256, 512), bf16),
    gqa=((D, 256), bf16),
    gqb=((D, 256), bf16),
    wdot=((D, HEAD), f32),
    ggu=((D, 768), bf16),
    go=((256, D), bf16),
    gd=((384, D), bf16),
    rqa=((16, 64, 256), bf16),
    rqb=((16, 64, 256), bf16),
    rgu=((16, 64, 768), bf16),
    ro=((16, 32, 512), bf16),
    rd=((16, 48, 512), bf16),
    sqa=((64, 256), bf16),
    sqb=((64, 256), bf16),
    sgu=((64, 768), bf16),
    so=((32, 512), bf16),
    sd=((48, 512), bf16),
    fqa=((8, 64, 256), bf16),
    fqb=((8, 64, 256), bf16),
    fgu=((8, 64, 768), bf16),
    fo=((128, D), bf16),
    fd=((192, D), bf16),
    dg=((24, 128), f32),
    dg_r1=((8, 24, 128), f32),
    dg_s=((24, 128), f32),
    dg_r2=((16, 24, 128), f32),
)
SEMAPHORES = dict(
    ld=16,
    s_x=7, r_x=7,
    s_dy=7, r_dy=7,
    s_n2=14, r_n2=14,
    s_dob=14, r_dob=14,
    s_pos=1, r_pos=1,
    s_gain=12, r_gain=12,
    s_wq=12, r_wq=12,
    s_wgu=12, r_wgu=12,
    s_wo=4, r_wo=1, s_wd=4, r_wd=1,
    s_wo2=8, r_wo2=8, s_wd2=8, r_wd2=8,
    s_kv=8, r_kv=8,
    s_c=32, r_c=32,
    s_r=24, r_r=24,
    s_dkv=2, r_dkv=2,
    s_gqa=16, r_gqa=16,
    s_gqb=16, r_gqb=16,
    s_ggu=16, r_ggu=16,
    s_go=16, r_go=16,
    s_gd=16, r_gd=16,
    s_fqa=8, r_fqa=8,
    s_fqb=8, r_fqb=8,
    s_fgu=8, r_fgu=8,
    s_fo=8, r_fo=8,
    s_fd=8, r_fd=8,
    s_dg1=8, r_dg1=8,
    s_dg2=16, r_dg2=16,
)


def dot(a, b):
    return jnp.dot(a, b, preferred_element_type=f32)


def dot_nt(a, b):
    return lax.dot_general(a, b, (((1,), (1,)), ((), ())), preferred_element_type=f32)


def dot_tn(a, b):
    return lax.dot_general(a, b, (((0,), (0,)), ((), ())), preferred_element_type=f32)


def to_row(g, first, count):
    return jnp.concatenate([g[first + i : first + i + 1, :] for i in range(count)], axis=1)


def layer_kernel(*refs):
    names = [*INPUTS, *OUTPUTS, *BUFFERS, *SEMAPHORES]
    r = types.SimpleNamespace(**dict(zip(names, refs, strict=True)))

    c = lax.axis_index("ctx")
    f = lax.axis_index("fsdp")
    xh, y = lax.div(c, 4), lax.rem(c, 4)
    xl, z, k = lax.div(f, 8), lax.rem(lax.div(f, 2), 4), lax.rem(f, 2)
    x = 2 * xh + xl
    part = 4 * xl + z
    t = 2 * y + k
    other = 1 - k

    def place(xh_, xl_, y_, z_, k_):
        return (xh_ * 4 + y_, xl_ * 8 + z_ * 2 + k_)

    partner = place(xh, xl, y, z, other)

    def around(value, step):
        return lax.rem(value + step, 4)

    def copy(src, dst, ss, rs, device):
        return pltpu.make_async_remote_copy(
            src_ref=src, dst_ref=dst, send_sem=ss, recv_sem=rs,
            device_id=device, device_id_type=MESH,
        )

    def send(src, dst, ss, rs, device):
        copy(src, dst, ss, rs, device).start()

    def got(ref, rs):
        copy(ref, ref, rs, rs, partner).wait_recv()

    def sent(ref, ss):
        copy(ref, ref, ss, ss, partner).wait_send()

    loads = []

    def load(src, dst):
        one = pltpu.make_async_copy(src, dst, r.ld.at[len(loads)])
        one.start()
        loads.append(one)

    for i in range(2):
        ti = 2 * y + i
        load(r.wqkv_f.at[:, pl.ds(pl.multiple_of(256 * ti, 256), 256)], r.wq_f.at[i, :, pl.ds(0, 256)])
        load(r.wqkv_f.at[:, pl.ds(pl.multiple_of(2048 + 128 * ti, 128), 128)], r.wq_f.at[i, :, pl.ds(256, 128)])
        load(r.wqkv_f.at[:, pl.ds(pl.multiple_of(3072 + 128 * ti, 128), 128)], r.wq_f.at[i, :, pl.ds(384, 128)])
    for i in range(2):
        ti = 2 * y + i
        load(r.wgu_f.at[:, pl.ds(pl.multiple_of(384 * ti, 128), 384)], r.wgu_fs.at[i, :, pl.ds(0, 384)])
        load(r.wgu_f.at[:, pl.ds(pl.multiple_of(3072 + 384 * ti, 128), 384)], r.wgu_fs.at[i, :, pl.ds(384, 384)])

    barrier = pltpu.get_barrier_semaphore()

    def greet(device):
        pl.semaphore_signal(barrier, inc=1, device_id=device, device_id_type=MESH)

    def greet_groups(i, carry):
        a, b, d = lax.div(i, 8), lax.rem(lax.div(i, 2), 4), lax.rem(i, 2)
        core = lax.rem(k + d, 2)
        greet(place(lax.rem(xh + a, 2), xl, around(y, b), z, core))
        greet(place(xh, lax.rem(xl + a, 2), y, around(z, b), core))
        x_ = lax.rem(x + lax.div(i, 4), 4)
        greet(place(lax.div(x_, 2), lax.rem(x_, 2), y, around(z, lax.rem(i, 4)), k))
        return carry

    home = (xl == lax.div(t, 4)) & (z == lax.rem(t, 4)) & (k == xl)

    def greet_senders(i, carry):
        @pl.when(jnp.logical_not(home & (lax.div(i, 4) == xh) & (lax.rem(i, 4) == z)))
        def _():
            greet(place(lax.div(i, 4), k, lax.div(part, 2), lax.rem(i, 4), lax.rem(part, 2)))

        return carry

    lax.fori_loop(1, 16, greet_groups, 0)
    lax.fori_loop(0, 8, greet_senders, 0)
    pl.semaphore_wait(barrier, 53 - home.astype(jnp.int32))

    def rows_of(half):
        return pl.ds(0, 128) if half is None else pl.ds(64 * half, 64)

    def gather_start(src, whole, ss, rs, half=None):
        rows, o = rows_of(half), 7 * (half or 0)
        for d in (1, 3, 2):
            send(src.at[rows], whole.at[y, k, rows], ss.at[o + d - 1], rs.at[o + d - 1], place(xh, xl, around(y, d), z, k))
        send(src.at[rows], whole.at[y, k, rows], ss.at[o + 3], rs.at[o + 3], partner)

    def gather_forward(whole, ss, rs, d, half=None):
        rows, o = rows_of(half), 7 * (half or 0)
        block = whole.at[around(y, 4 - d), k, rows]
        got(block, rs.at[o + d - 1])
        send(block, block, ss.at[o + 3 + d], rs.at[o + 3 + d], partner)

    def gather_own(whole, rs, half=None):
        got(whole.at[y, other, rows_of(half)], rs.at[7 * (half or 0) + 3])

    def gather_pair(whole, rs, d, half=None):
        got(whole.at[around(y, 4 - d), other, rows_of(half)], rs.at[7 * (half or 0) + 3 + d])

    def gather_end(whole, ss, half=None):
        for i in range(7):
            sent(whole.at[y, k, rows_of(half)], ss.at[7 * (half or 0) + i])

    def chip_slots(whole, l_, zz):
        return whole.at[pl.ds(8 * l_ + 2 * zz, 2)]

    def z_send(src_of, whole, ss, rs):
        for i in range(1, 8):
            core = lax.rem(k + i, 2)
            send(src_of(core), whole.at[f], ss.at[i], rs.at[i], place(xh, xl, y, around(z, i // 2), core))

    def z_got(whole, rs, dz):
        for dk in range(2):
            if dz + dk > 0:
                got(whole.at[8 * xl + 2 * around(z, 4 - dz) + lax.rem(k + dk, 2)], rs.at[2 * dz + dk])

    def beside(dz):
        x_ = around(x, 1 if dz < 2 else 3)
        return place(lax.div(x_, 2), lax.rem(x_, 2), y, z, k)

    def x_send(whole, ss, rs, dz):
        block = chip_slots(whole, xl, around(z, 4 - dz))
        send(block, block, ss.at[8 + dz], rs.at[8 + dz], beside(dz))

    def x_got(whole, rs, dz):
        got(chip_slots(whole, 1 - xl, around(z, 4 - dz)), rs.at[8 + dz])

    def rows_sent(whole, ss):
        for i in range(1, 8):
            sent(whole.at[f], ss.at[i])
        for dz in range(4):
            sent(chip_slots(whole, xl, around(z, 4 - dz)), ss.at[8 + dz])

    def loop_sent(ref, ss, first, last):
        def one(i, carry):
            sent(ref, ss.at[i])
            return carry

        lax.fori_loop(first, last, one, 0)

    gather_start(r.tok, r.x_all, r.s_x, r.r_x)
    send(r.pos_in, r.pos.at[k], r.s_pos.at[0], r.r_pos.at[0], partner)
    for one in loads[:6]:
        one.wait()
    r.wq_send[...] = r.wq_f[...].astype(bf16)
    z_send(lambda k_: r.wq_send.at[k_], r.wq, r.s_wq, r.r_wq)
    z_send(lambda k_: r.gain_in, r.gain_recv, r.s_gain, r.r_gain)
    r.wq[f] = r.wq_send[k]
    r.gain_recv[f] = r.gain_in[...]

    r.wo_own[...] = r.wo_f[...].astype(bf16)
    r.wd_own[...] = r.wd_f[...].astype(bf16)
    is_source = lax.div(part, 2) == y
    to_core = lax.rem(part, 2)
    for i in range(4):
        piece = 4 * k + i
        here = (xl == k) & (z == i) & (to_core == k)

        @pl.when(is_source & jnp.logical_not(here))
        def _():
            there = place(xh, k, y, i, to_core)
            send(r.wo_own.at[pl.ds(32 * i, 32)], r.wo.at[pl.ds(pl.multiple_of(32 * piece, 32), 32)], r.s_wo.at[i], r.r_wo.at[0], there)
            send(r.wd_own.at[pl.ds(48 * i, 48)], r.wd.at[pl.ds(pl.multiple_of(48 * piece, 16), 48)], r.s_wd.at[i], r.r_wd.at[0], there)

        @pl.when(is_source & here)
        def _():
            r.wo[pl.ds(pl.multiple_of(32 * piece, 32), 32), :] = r.wo_own[32 * i : 32 * i + 32, :]
            r.wd[pl.ds(pl.multiple_of(48 * piece, 16), 48), :] = r.wd_own[48 * i : 48 * i + 48, :]

    def wo_rows(q):
        return r.wo.at[pl.ds(pl.multiple_of(32 * q, 32), 32)]

    def wd_rows(q):
        return r.wd.at[pl.ds(pl.multiple_of(48 * q, 16), 48)]

    r.x_all[y, k] = r.tok[...]
    r.dy_all[y, k] = r.dyt[...]
    r.pos[k] = r.pos_in[...]
    for one in loads[6:]:
        one.wait()
    r.wgu_send[...] = r.wgu_fs[...].astype(bf16)
    r.wgu[f] = r.wgu_send[k]

    got(r.pos.at[other], r.r_pos.at[0])
    steps = lax.broadcasted_iota(jnp.int32, (BLOCK, 1), 0).astype(f32)
    for s in range(2):
        for b in range(16):
            r.posk[s, b * BLOCK : (b + 1) * BLOCK, :] = r.pos[s, 0:1, b * BLOCK : b * BLOCK + 1] + steps
    freq = r.freq[0:1, :]
    sign = r.freq[1:2, :]

    def tables(yy, carry):
        for s in range(2):
            rows = r.posk[s, pl.ds(pl.multiple_of(512 * xh + 128 * yy, 128), 128), :]
            angle = rows * freq
            r.cos_t[yy, s * 128 : (s + 1) * 128, :] = jnp.cos(angle)
            r.sin_t[yy, s * 128 : (s + 1) * 128, :] = jnp.sin(angle) * sign
        return carry

    lax.fori_loop(0, 4, tables, 0)

    for dz in (0, 1, 3, 2):
        z_got(r.gain_recv, r.r_gain, dz)
        x_send(r.gain_recv, r.s_gain, r.r_gain, dz)
        z_got(r.wq, r.r_wq, dz)
        x_send(r.wq, r.s_wq, r.r_wq, dz)
    z_send(lambda k_: r.wgu_send.at[k_], r.wgu, r.s_wgu, r.r_wgu)
    gather_start(r.dyt, r.dy_all, r.s_dy, r.r_dy)
    own_piece = (2 * y + k == part) & (xl == k)

    @pl.when(jnp.logical_not(own_piece))
    def _():
        got(wo_rows(part), r.r_wo.at[0])
        got(wd_rows(part), r.r_wd.at[0])

    for dz in range(1, 4):
        there = place(xh, xl, y, around(z, dz), k)
        send(wo_rows(part), wo_rows(part), r.s_wo2.at[dz], r.r_wo2.at[dz], there)
        send(wd_rows(part), wd_rows(part), r.s_wd2.at[dz], r.r_wd2.at[dz], there)

    def piece_of(l_, dz):
        return 4 * l_ + around(z, 4 - dz)

    for dz in range(4):
        x_got(r.gain_recv, r.r_gain, dz)
    gains = jnp.sum(r.gain_recv[...], axis=0)
    g1 = to_row(gains, 0, 8)
    g2 = to_row(gains, 8, 8)
    gq = gains[16:17, :]
    gk = gains[17:18, :]

    def rotated(u, cos, sin):
        return u * cos + pltpu.roll(u, 64, 1) * sin

    def unrotated(u, cos, sin):
        return u * cos - pltpu.roll(u, 64, 1) * sin

    def inverse_rms(u):
        return lax.rsqrt(jnp.mean(u * u, axis=-1, keepdims=True) + norm_eps)

    kv_partner = place(1 - xh, xl, y, z, k)

    def kv_rows(s, hh, yy):
        return r.kv.at[s, pl.ds(pl.multiple_of(512 * hh + 128 * yy, 128), 128)]

    def project(d):
        yy = around(y, 4 - d)
        rows = r.x_all[yy].reshape(256, D).astype(f32)
        n1 = (rows * inverse_rms(rows) * g1).astype(bf16)
        r.n1_all[yy] = n1
        qkv = dot(n1, r.wq[...].reshape(D, 512))
        r.qkraw[yy] = qkv[:, :384]
        cos, sin = r.cos_t[yy], r.sin_t[yy]
        local = pl.ds(pl.multiple_of(512 * xh + 128 * yy, 128), 128)
        u = qkv[:, 256:384]
        u = rotated(u * inverse_rms(u) * gk, cos, sin).astype(bf16)
        v = qkv[:, 384:].astype(bf16)
        for s in range(2):
            r.kv[s, local, 0:HEAD] = u[s * 128 : (s + 1) * 128]
            r.kv[s, local, HEAD : 2 * HEAD] = v[s * 128 : (s + 1) * 128]
            send(kv_rows(s, xh, yy), kv_rows(s, xh, yy), r.s_kv.at[2 * d + s], r.r_kv.at[2 * d + s], kv_partner)
        for h in range(2):
            u = qkv[:, h * HEAD : (h + 1) * HEAD]
            u = rotated(u * inverse_rms(u) * gq, cos, sin).astype(bf16)
            for s in range(2):
                for half in range(2):
                    first = s * 128 + half * 64
                    r.q_s[s, half, pl.ds(pl.multiple_of(64 * yy, 64), 64), h * HEAD : (h + 1) * HEAD] = u[first : first + 64]

    gather_own(r.x_all, r.r_x)
    for d in (1, 3):
        gather_forward(r.x_all, r.s_x, r.r_x, d)
    for dz in range(4):
        x_got(r.wq, r.r_wq, dz)
    project(0)
    gather_pair(r.x_all, r.r_x, 1)
    project(1)
    gather_forward(r.x_all, r.s_x, r.r_x, 2)
    gather_pair(r.x_all, r.r_x, 3)
    project(3)
    gather_pair(r.x_all, r.r_x, 2)
    project(2)
    gather_end(r.x_all, r.s_x)

    for dz in range(4):
        if dz > 0:
            got(wo_rows(piece_of(xl, dz)), r.r_wo2.at[dz])
        block = wo_rows(piece_of(xl, dz))
        send(block, block, r.s_wo2.at[4 + dz], r.r_wo2.at[4 + dz], beside(dz))
    for dz in range(4):
        z_got(r.wgu, r.r_wgu, dz)
        x_send(r.wgu, r.s_wgu, r.r_wgu, dz)
    for dz in range(4):
        if dz > 0:
            got(wd_rows(piece_of(xl, dz)), r.r_wd2.at[dz])
        block = wd_rows(piece_of(xl, dz))
        send(block, block, r.s_wd2.at[4 + dz], r.r_wd2.at[4 + dz], beside(dz))
    for d in (1, 3, 2):
        gather_forward(r.dy_all, r.s_dy, r.r_dy, d)

    for d in (0, 1, 3, 2):
        for s in range(2):
            got(kv_rows(s, 1 - xh, around(y, 4 - d)), r.r_kv.at[2 * d + s])

    def lanes(half):
        return pl.ds(pl.multiple_of(256 * half, 256), 256)

    def allowed(s, half):
        return r.posk[s] <= r.pos[s, 1:2, lanes(half)]

    def attend(half):
        def one(s, carry):
            ok = allowed(s, half)
            for h in range(2):
                q = r.q_s[s, half, :, h * HEAD : (h + 1) * HEAD]
                scores = jnp.where(ok, dot_nt(r.kv[s, :, 0:HEAD], q) * SCALE, -1e30)
                top = jnp.max(scores, axis=0, keepdims=True)
                p = jnp.exp(scores - top)
                total = jnp.sum(p, axis=0, keepdims=True)
                o = dot_tn(r.kv[s, :, HEAD : 2 * HEAD], p.astype(bf16)) / total
                r.o_t[s, h * HEAD : (h + 1) * HEAD, lanes(half)] = o
                r.ob_t[s, h * HEAD : (h + 1) * HEAD, lanes(half)] = o.astype(bf16)
                r.lse[s, h, :, lanes(half)] = top + jnp.log(total)
            return carry

        lax.fori_loop(0, 2, one, 0)

    def reduce_first(use, p, cc, d, half=None):
        yy, rows, i = around(y, d), rows_of(half), 8 * use + 4 * (half or 0) + d
        send(p.at[yy, other, rows], cc.at[yy, rows], r.s_c.at[i], r.r_c.at[i], partner)

    def both_cores(use, p, cc, d, half):
        yy, rows, i = around(y, d), rows_of(half), 8 * use + 4 * (half or 0) + d
        got(cc.at[yy, rows], r.r_c.at[i])
        return p[yy, k, rows, :].astype(f32) + cc[yy, rows, :].astype(f32)

    def reduce_second(use, p, cc, rr, d, half=None):
        yy, rows, i = around(y, d), rows_of(half), 6 * use + 3 * (half or 0) + d - 1
        p[yy, k, rows, :] = both_cores(use, p, cc, d, half).astype(bf16)
        send(p.at[yy, k, rows], rr.at[d - 1, rows], r.s_r.at[i], r.r_r.at[i], place(xh, xl, yy, z, k))

    def reduce_third(use, p, cc, rr, half=None):
        rows = rows_of(half)
        total = both_cores(use, p, cc, 0, half)
        for d in (1, 3, 2):
            got(rr.at[d - 1, rows], r.r_r.at[6 * use + 3 * (half or 0) + d - 1])
            total = total + rr[d - 1, rows, :].astype(f32)
        return total

    def reduce_end(use, p, half=None):
        rows = rows_of(half)
        for d in range(4):
            sent(p.at[y, other, rows], r.s_c.at[8 * use + 4 * (half or 0) + d])
        for d in range(3):
            sent(p.at[y, k, rows], r.s_r.at[6 * use + 3 * (half or 0) + d])

    def out_partial(half):
        for s in range(2):
            o = r.ob_t[s, :, lanes(half)]
            r.pa[:, s, rows_of(half), :] = dot_tn(o, r.wo[...]).astype(bf16).reshape(4, 64, D)
        for d in (2, 1, 3, 0):
            reduce_first(0, r.pa, r.ca, d, half)

    attend(0)
    for dz in range(4):
        got(wo_rows(piece_of(1 - xl, dz)), r.r_wo2.at[4 + dz])
    out_partial(0)
    attend(1)
    for d in (2, 1, 3):
        reduce_second(0, r.pa, r.ca, r.ra, d, 0)
    out_partial(1)
    for d in (2, 1, 3):
        reduce_second(0, r.pa, r.ca, r.ra, d, 1)
    for half in range(2):
        rows = rows_of(half)
        h1 = r.tok[rows, :].astype(f32) + reduce_third(0, r.pa, r.ca, r.ra, half)
        r.h1[rows, :] = h1
        r.n2_all[y, k, rows, :] = (h1 * inverse_rms(h1) * g2).astype(bf16)
        gather_start(r.n2_all.at[y, k], r.n2_all, r.s_n2, r.r_n2, half)

    gather_own(r.dy_all, r.r_dy)
    for d in (1, 3, 2):
        gather_pair(r.dy_all, r.r_dy, d)
    for dz in range(4):
        x_got(r.wgu, r.r_wgu, dz)
        got(wd_rows(piece_of(1 - xl, dz)), r.r_wd2.at[4 + dz])

    def two_blocks(whole, ds, half):
        blocks = [whole[around(y, d), :, rows_of(half), :].reshape(128, whole.shape[-1]) for d in ds]
        return jnp.concatenate(blocks, axis=0)

    def put_blocks(whole, ds, half, cols, value):
        for i, d in enumerate(ds):
            block = value[128 * i : 128 * (i + 1)].reshape(2, 64, value.shape[-1])
            whole[around(y, d), :, rows_of(half), cols] = block

    def feed(ds, half):
        n2 = two_blocks(r.n2_all, ds, half)
        ab = dot(n2, r.wgu[...].reshape(D, 768))
        a, b = ab[:, :384], ab[:, 384:]
        sig = jax.nn.sigmoid(a)
        silu = a * sig
        put_blocks(r.hid_all, ds, half, slice(None), (silu * b).astype(bf16))
        dhid = dot_nt(two_blocks(r.dy_all, ds, half), r.wd[...])
        da = (dhid * b * sig * (1.0 + a * (1.0 - sig))).astype(bf16)
        db = (dhid * silu).astype(bf16)
        put_blocks(r.dgu_all, ds, half, slice(0, 384), da)
        put_blocks(r.dgu_all, ds, half, slice(384, 768), db)
        dn2 = dot_nt(jnp.concatenate([da, db], axis=1), r.wgu[...].reshape(D, 768))
        put_blocks(r.pb, ds, half, slice(None), dn2.astype(bf16))
        for d in ds:
            reduce_first(1, r.pb, r.cb, d, half)

    for half in range(2):
        gather_own(r.n2_all, r.r_n2, half)
        for d in (1, 3):
            gather_forward(r.n2_all, r.s_n2, r.r_n2, d, half)
        gather_pair(r.n2_all, r.r_n2, 1, half)
        feed((0, 3), half)
        gather_forward(r.n2_all, r.s_n2, r.r_n2, 2, half)
        gather_pair(r.n2_all, r.r_n2, 3, half)
        gather_pair(r.n2_all, r.r_n2, 2, half)
        feed((2, 1), half)
        for d in (3, 2, 1):
            reduce_second(1, r.pb, r.cb, r.rb, d, half)

    def cross(i, sign):
        dx, dz = lax.div(i, 4), lax.rem(i, 4)
        x_, z_ = lax.rem(x + 4 + sign * dx, 4), lax.rem(z + 4 + sign * dz, 4)
        return lax.div(x_, 2), lax.rem(x_, 2), z_

    def cross_send(piece_of, dst, ss, rs):
        def one(i, carry):
            h_, l_, z_ = cross(i, 1)
            send(piece_of(h_, 4 * l_ + z_), dst.at[i], ss.at[i], rs.at[i], place(h_, l_, y, z_, k))
            return carry

        lax.fori_loop(1, 16, one, 0)

    def cross_sum(own, dst, rs):
        def one(i, total):
            got(dst.at[i], rs.at[i])
            return total + dst[i].astype(f32)

        return lax.fori_loop(1, 16, one, own.astype(f32))

    def piece_rows(whole, height):
        def of(h_, p_):
            return whole.at[pl.ds(pl.multiple_of(2 * height * p_ + height * h_, height), height)]

        return of

    def piece_block(whole, height):
        def of(h_, p_):
            return whole.at[pl.ds(pl.multiple_of(height * p_, 16), height), pl.ds(pl.multiple_of(512 * h_, 512), 512)]

        return of

    gqa_piece, gqb_piece, ggu_piece = piece_rows(r.gqa, 64), piece_rows(r.gqb, 64), piece_rows(r.ggu, 64)
    go_piece, gd_piece = piece_block(r.go, 32), piece_block(r.gd, 48)

    def weight_gradient(left, right, out):
        def one(i, carry):
            cols = pl.ds(pl.multiple_of(256 * i, 256), 256)
            out[:, cols] = dot_tn(left(), right(cols)).astype(bf16)
            return carry

        lax.fori_loop(0, out.shape[1] // 256, one, 0)

    r.dg[...] = jnp.zeros((24, 128), f32)

    def middle_back(half):
        rows = rows_of(half)
        dn2 = reduce_third(1, r.pb, r.cb, r.rb, half)
        h1 = r.h1[rows, :]
        r2 = inverse_rms(h1)
        weighted = dn2 * g2
        back = r2 * weighted - h1 * (r2 * r2 * r2) * jnp.mean(weighted * h1, axis=-1, keepdims=True)
        dh1 = r.dyt[rows, :].astype(f32) + back
        r.dh1[rows, :] = dh1
        dg2 = jnp.sum(dn2 * h1 * r2, axis=0, keepdims=True)
        for i in range(8):
            r.dg[8 + i : 9 + i, :] += dg2[:, 128 * i : 128 * (i + 1)]
        r.x_all[y, k, rows, :] = dh1.astype(bf16)
        gather_start(r.x_all.at[y, k], r.x_all, r.s_dob, r.r_dob, half)

    weight_gradient(
        lambda: r.hid_all[...].reshape(D, 384),
        lambda cols: r.dy_all[:, :, :, cols].reshape(D, 256),
        r.gd,
    )
    cross_send(gd_piece, r.rd, r.s_gd, r.r_gd)
    middle_back(0)
    weight_gradient(
        lambda: r.n2_all[...].reshape(D, D),
        lambda cols: r.dgu_all[:, :, :, cols].reshape(D, 256),
        r.ggu,
    )
    middle_back(1)
    cross_send(ggu_piece, r.rgu, r.s_ggu, r.r_ggu)

    def norm_back(value, gain, grad):
        inverse = inverse_rms(value)
        w = grad * gain
        back = inverse * w - value * (inverse * inverse * inverse) * jnp.mean(w * value, axis=-1, keepdims=True)
        return back, jnp.sum(grad * value * inverse, axis=0, keepdims=True)

    def attend_back(half, s):
        rows = rows_of(half)
        do_s = dot_nt(r.wo[...], r.x_all[:, s, rows, :].reshape(256, D)).astype(bf16)
        prod = do_s.astype(f32) * r.o_t[s, :, lanes(half)]
        r.do_t[s, :, lanes(half)] = do_s
        ok = allowed(s, half)
        keys, values = r.kv[s, :, 0:HEAD], r.kv[s, :, HEAD : 2 * HEAD]
        mine = pl.ds(s * 128 + 64 * half, 64)
        cos = r.cos_t[:, mine, :].reshape(256, HEAD)
        sin = r.sin_t[:, mine, :].reshape(256, HEAD)
        for h in range(2):
            head = slice(h * HEAD, (h + 1) * HEAD)
            q = r.q_s[s, half, :, head]
            do = r.do_t[s, head, lanes(half)]
            delta = jnp.sum(prod[head], axis=0, keepdims=True)
            scores = dot_nt(keys, q) * SCALE
            p = jnp.where(ok, jnp.exp(scores - r.lse[s, h, :, lanes(half)]), 0.0)
            ds = (p * (dot(values, do) - delta)).astype(bf16)
            dv = dot_nt(p.astype(bf16), do)
            dk = dot(ds, q) * SCALE
            if half == 0 and h == 0:
                r.dkv[s, :, HEAD : 2 * HEAD] = dv
                r.dkv[s, :, 0:HEAD] = dk
            else:
                r.dkv[s, :, HEAD : 2 * HEAD] += dv
                r.dkv[s, :, 0:HEAD] += dk
            dq = (dot_tn(keys, ds) * SCALE).T
            raw = r.qkraw[:, mine, head].reshape(256, HEAD)
            back, gain_grad = norm_back(raw, gq, unrotated(dq, cos, sin))
            r.dqkv[:, mine, head] = back.astype(bf16).reshape(4, 64, HEAD)
            r.dg[16:17, :] += gain_grad

    def gather_rest(half):
        gather_own(r.x_all, r.r_dob, half)
        for d in (1, 3, 2):
            gather_forward(r.x_all, r.s_dob, r.r_dob, d, half)
        for d in (1, 3, 2):
            gather_pair(r.x_all, r.r_dob, d, half)

    for half in range(2):
        reduce_end(0, r.pa, half)

    def down_partial(i, carry):
        hid = r.hid_all[i].reshape(256, 384)
        r.pa[i] = dot(hid, r.wd[...]).astype(bf16).reshape(2, 128, D)
        return carry

    lax.fori_loop(0, 4, down_partial, 0)
    for d in (2, 1, 3, 0):
        reduce_first(2, r.pa, r.ca, d)
    gather_rest(0)
    for s in range(2):
        attend_back(0, s)
    gather_rest(1)
    for d in (2, 1, 3):
        reduce_second(2, r.pa, r.ca, r.ra, d)
    for s in range(2):
        attend_back(1, s)
        r.dkv_send[s] = r.dkv[s, pl.ds(pl.multiple_of(512 * (1 - xh), 512), 512), :].astype(bf16)
        send(r.dkv_send.at[s], r.dkv_recv.at[s], r.s_dkv.at[s], r.r_dkv.at[s], kv_partner)

    def qkv_gradient(first, out):
        grad = dot_tn(r.n1_all[...].reshape(D, D), r.dqkv[:, :, first : first + 256].reshape(D, 256))
        out[...] = grad.astype(bf16)
        prod = grad * r.wq[:, :, first : first + 256].reshape(D, 256).astype(f32)
        return prod[:, 0:128] + prod[:, 128:256]

    r.wdot[...] = qkv_gradient(0, r.gqa)
    cross_send(gqa_piece, r.rqa, r.s_gqa, r.r_gqa)

    def out_gradient(i, carry):
        cols = pl.ds(pl.multiple_of(256 * i, 256), 256)
        total = jnp.zeros((256, 256), f32)
        for s in range(2):
            for half in range(2):
                rows = r.x_all[:, s, rows_of(half), cols].reshape(256, 256)
                total = total + dot(r.ob_t[s, :, lanes(half)], rows)
        r.go[:, cols] = total.astype(bf16)
        return carry

    lax.fori_loop(0, 4, out_gradient, 0)
    cross_send(go_piece, r.ro, r.s_go, r.r_go)

    def spread_rows(total, hold, final, ss, rs):
        hold[...] = total.astype(bf16)

        def one(i, carry):
            there = place(lax.rem(xh + lax.div(i, 4), 2), xl, lax.rem(y + i, 4), z, xh)

            @pl.when((i > 0) | (k != xh))
            def _():
                send(hold, final.at[t], ss.at[i], rs.at[t], there)

            return carry

        lax.fori_loop(0, 8, one, 0)

        @pl.when(k == xh)
        def _():
            final[t] = hold[...]

    def spread_rows_sent(hold, ss):
        def one(i, carry):
            @pl.when((i > 0) | (k != xh))
            def _():
                sent(hold, ss.at[i])

            return carry

        lax.fori_loop(0, 8, one, 0)

    def spread_rows_got(final, rs):
        def one(i, carry):
            @pl.when((i != t) | (k != xh))
            def _():
                got(final.at[i], rs.at[i])

            return carry

        lax.fori_loop(0, 8, one, 0)

    def spread_block(total, hold, final, height, ss, rs):
        hold[...] = total.astype(bf16)
        rows = pl.ds(pl.multiple_of(height * z, 16), height)
        cols = pl.ds(pl.multiple_of(512 * xh, 512), 512)

        def one(i, carry):
            there = place(lax.rem(xh + lax.div(i, 4), 2), lax.div(t, 4), lax.rem(y + i, 4), lax.rem(t, 4), xl)

            @pl.when((i > 0) | jnp.logical_not(home))
            def _():
                send(hold, final.at[rows, cols], ss.at[i], rs.at[4 * xh + z], there)

            return carry

        lax.fori_loop(0, 8, one, 0)

        @pl.when(home)
        def _():
            final[rows, cols] = hold[...]

    def spread_block_sent(hold, ss):
        def one(i, carry):
            @pl.when((i > 0) | jnp.logical_not(home))
            def _():
                sent(hold, ss.at[i])

            return carry

        lax.fori_loop(0, 8, one, 0)

    def spread_block_got(final, height, rs):
        def one(i, carry):
            @pl.when((i != 4 * xh + z) | jnp.logical_not(home))
            def _():
                rows = pl.ds(pl.multiple_of(height * lax.rem(i, 4), 16), height)
                cols = pl.ds(pl.multiple_of(512 * lax.div(i, 4), 512), 512)
                got(final.at[rows, cols], rs.at[i])

            return carry

        lax.fori_loop(0, 8, one, 0)

    spread_block(cross_sum(gd_piece(xh, part)[...], r.rd, r.r_gd), r.sd, r.fd, 48, r.s_fd, r.r_fd)
    spread_rows(cross_sum(ggu_piece(xh, part)[...], r.rgu, r.r_ggu), r.sgu, r.fgu, r.s_fgu, r.r_fgu)

    for half in range(2):
        reduce_end(1, r.pb, half)
    for s in range(2):
        got(r.dkv_recv.at[s], r.r_dkv.at[s])

    def key_back(yy, carry):
        rows = pl.ds(pl.multiple_of(512 * xh + 128 * yy, 128), 128)
        local = pl.ds(pl.multiple_of(128 * yy, 128), 128)
        grads = [r.dkv[s, rows, :] + r.dkv_recv[s, local, :].astype(f32) for s in range(2)]
        both = jnp.concatenate(grads, axis=0)
        du = unrotated(both[:, 0:HEAD], r.cos_t[yy], r.sin_t[yy])
        back, gain_grad = norm_back(r.qkraw[yy, :, 256:384], gk, du)
        r.dqkv[yy, :, 256:384] = back.astype(bf16)
        r.dqkv[yy, :, 384:512] = both[:, HEAD : 2 * HEAD].astype(bf16)
        r.dg[17:18, :] += gain_grad
        return carry

    lax.fori_loop(0, 4, key_back, 0)
    for d in (2, 1, 3, 0):
        yy = around(y, d)
        dn1 = dot_nt(r.dqkv[yy], r.wq[...].reshape(D, 512))
        r.pb[yy] = dn1.astype(bf16).reshape(2, 128, D)
        reduce_first(3, r.pb, r.cb, d)
    wdot = r.wdot[...] + qkv_gradient(256, r.gqb)
    cross_send(gqb_piece, r.rqb, r.s_gqb, r.r_gqb)
    for d in (2, 1, 3):
        reduce_second(3, r.pb, r.cb, r.rb, d)
    dg1 = jnp.sum(wdot.T, axis=0, keepdims=True) / g1
    for i in range(8):
        r.dg[i : i + 1, :] = dg1[:, 128 * i : 128 * (i + 1)]
    for i in range(1, 8):
        there = place(xh, xl, around(y, i // 2), z, lax.rem(k + i, 2))
        send(r.dg, r.dg_r1.at[i], r.s_dg1.at[i], r.r_dg1.at[i], there)

    spread_rows(cross_sum(gqa_piece(xh, part)[...], r.rqa, r.r_gqa), r.sqa, r.fqa, r.s_fqa, r.r_fqa)
    spread_block(cross_sum(go_piece(xh, part)[...], r.ro, r.r_go), r.so, r.fo, 32, r.s_fo, r.r_fo)
    out_tokens = r.h1[...] + reduce_third(2, r.pa, r.ca, r.ra)
    r.out_tok[...] = out_tokens.astype(bf16)
    total = r.dg[...]
    for i in range(1, 8):
        got(r.dg_r1.at[i], r.r_dg1.at[i])
        total = total + r.dg_r1[i]
    r.dg_s[...] = total
    cross_send(lambda h_, p_: r.dg_s, r.dg_r2, r.s_dg2, r.r_dg2)
    spread_rows(cross_sum(gqb_piece(xh, part)[...], r.rqb, r.r_gqb), r.sqb, r.fqb, r.s_fqb, r.r_fqb)

    dn1 = reduce_third(3, r.pb, r.cb, r.rb)
    rows = r.tok[...].astype(f32)
    back, unused = norm_back(rows, g1, dn1)
    r.dtok[...] = (r.dh1[...] + back).astype(bf16)

    spread_block_got(r.fd, 48, r.r_fd)
    r.g_dn[...] = r.fd[...]
    spread_rows_got(r.fgu, r.r_fgu)
    for i in range(8):
        r.g_gu[:, 384 * i : 384 * (i + 1)] = r.fgu[i, :, 0:384]
        r.g_gu[:, 3072 + 384 * i : 3072 + 384 * (i + 1)] = r.fgu[i, :, 384:768]
    spread_block_got(r.fo, 32, r.r_fo)
    r.g_out[...] = r.fo[...]
    spread_rows_got(r.fqa, r.r_fqa)
    for i in range(8):
        r.g_qkv[:, 256 * i : 256 * (i + 1)] = r.fqa[i]
    r.g_gain[...] = cross_sum(r.dg_s[...], r.dg_r2, r.r_dg2)
    spread_rows_got(r.fqb, r.r_fqb)
    for i in range(8):
        r.g_qkv[:, 2048 + 128 * i : 2048 + 128 * (i + 1)] = r.fqb[i, :, 0:128]
        r.g_qkv[:, 3072 + 128 * i : 3072 + 128 * (i + 1)] = r.fqb[i, :, 128:256]

    gather_end(r.dy_all, r.s_dy)
    for half in range(2):
        gather_end(r.n2_all, r.s_n2, half)
        gather_end(r.x_all, r.s_dob, half)
    sent(r.pos_in, r.s_pos.at[0])
    for whole, ss in ((r.gain_recv, r.s_gain), (r.wq, r.s_wq), (r.wgu, r.s_wgu)):
        rows_sent(whole, ss)
    for i in range(4):
        here = (xl == k) & (z == i) & (to_core == k)

        @pl.when(is_source & jnp.logical_not(here))
        def _():
            sent(r.wo_own.at[pl.ds(32 * i, 32)], r.s_wo.at[i])
            sent(r.wd_own.at[pl.ds(48 * i, 48)], r.s_wd.at[i])

    loop_sent(wo_rows(part), r.s_wo2, 1, 8)
    loop_sent(wd_rows(part), r.s_wd2, 1, 8)
    loop_sent(r.kv.at[0, pl.ds(0, 128)], r.s_kv, 0, 8)
    reduce_end(2, r.pa)
    reduce_end(3, r.pb)
    for s in range(2):
        sent(r.dkv_send.at[s], r.s_dkv.at[s])
    loop_sent(gqa_piece(xh, part), r.s_gqa, 1, 16)
    loop_sent(gqb_piece(xh, part), r.s_gqb, 1, 16)
    loop_sent(ggu_piece(xh, part), r.s_ggu, 1, 16)
    loop_sent(go_piece(xh, part), r.s_go, 1, 16)
    loop_sent(gd_piece(xh, part), r.s_gd, 1, 16)
    spread_rows_sent(r.sqa, r.s_fqa)
    spread_rows_sent(r.sqb, r.s_fqb)
    spread_rows_sent(r.sgu, r.s_fgu)
    spread_block_sent(r.so, r.s_fo)
    spread_block_sent(r.sd, r.s_fd)
    loop_sent(r.dg, r.s_dg1, 1, 8)
    loop_sent(r.dg_s, r.s_dg2, 1, 16)


def layer(*args):
    vmem = pl.BlockSpec(memory_space=pltpu.VMEM)
    hbm = pl.BlockSpec(memory_space=pl.ANY)
    specs = [hbm if far else vmem for far in INPUTS.values()]
    return pl.pallas_call(
        layer_kernel,
        out_shape=[jax.ShapeDtypeStruct(shape, kind) for shape, kind in OUTPUTS.values()],
        in_specs=specs,
        out_specs=[vmem] * len(OUTPUTS),
        scratch_shapes=[pltpu.VMEM(shape, kind) for shape, kind in BUFFERS.values()]
        + [pltpu.SemaphoreType.DMA((count,)) for count in SEMAPHORES.values()],
        compiler_params=pltpu.CompilerParams(
            collective_id=0, has_side_effects=True, vmem_limit_bytes=62 << 20
        ),
        name="layer",
    )(*args)


def adam_update(weight, moment, square, grad, rate, decay):
    moment_new = beta_first * moment + (1.0 - beta_first) * grad
    square_new = beta_second * square + (1.0 - beta_second) * grad * grad
    fix_first = 1.0 - beta_first**STEP
    fix_second = 1.0 - beta_second**STEP
    step = moment_new / fix_first / (jnp.sqrt(square_new / fix_second) + adam_eps)
    return (weight - rate * (step + decay * weight), moment_new, square_new)


def on_device(
    tokens, d_out, block_ids,
    w_qkv, w_out, w_gate_up, w_down, gains,
    moment_qkv, moment_out, moment_gate_up, moment_down, moment_gains,
    square_qkv, square_out, square_gate_up, square_down, square_gains,
):
    f = lax.axis_index("fsdp")
    starts = block_ids[0].astype(f32) * BLOCK
    spots = starts[:, None] + jnp.arange(BLOCK, dtype=f32)[None, :]
    mine = lax.dynamic_slice(spots, (8 * lax.div(lax.axis_index("ctx"), 4), 0), (8, BLOCK))
    mine = mine.reshape(4, 2, BLOCK).transpose(1, 0, 2).reshape(1, 512)
    positions = jnp.concatenate([spots.reshape(1, D), jnp.tile(mine, (7, 2))], axis=0)
    gain_rows = lax.dynamic_update_slice(
        jnp.zeros((24 * 128,), f32), gains.astype(bf16).astype(f32), (f * 144,)
    ).reshape(24, 128)
    half = rope_base ** (-(np.arange(64, dtype=np.float32) * np.float32(2.0 / HEAD)))
    table = np.zeros((8, 128), np.float32)
    table[0] = np.concatenate([half, half])
    table[1] = np.concatenate([-np.ones(64), np.ones(64)])
    out_tok, dtok, g_qkv, g_out, g_gu, g_dn, g_gain = layer(
        tokens[0], d_out[0], positions, gain_rows, jnp.asarray(table), w_qkv, w_out, w_gate_up, w_down
    )
    grad_gains = lax.dynamic_slice(g_gain.reshape(24 * 128), (f * 144,), (144,))
    grads = (g_qkv, g_out, g_gu, g_dn, grad_gains)
    masters = (w_qkv, w_out, w_gate_up, w_down, gains)
    moments = (moment_qkv, moment_out, moment_gate_up, moment_down, moment_gains)
    squares = (square_qkv, square_out, square_gate_up, square_down, square_gains)
    rates = (0.03, 0.3, 0.03, 0.03, 0.5)
    decays = (decay_rate, decay_rate, decay_rate, decay_rate, 0.0)
    updates = [
        adam_update(masters[i], moments[i], squares[i], grads[i].astype(f32), rates[i], decays[i])
        for i in range(5)
    ]
    return (
        out_tok[None],
        dtok[None],
        *(u[0] for u in updates),
        *(u[1] for u in updates),
        *(u[2] for u in updates),
    )


def solution(mesh):
    rows, flat = P("fsdp", None), P("fsdp")
    tokens = P("fsdp", "ctx", None)
    state = (rows, rows, rows, rows, flat)
    return jax.shard_map(
        on_device,
        mesh=mesh,
        in_specs=(tokens, tokens, rows) + state * 3,
        out_specs=(tokens, tokens) + state * 3,
        check_vma=False,
    )
```

profile of v0, /device:TPU:1, one launch (start us, length us, event | category | flops | bytes accessed | tf_op | source)
XLA Modules:
  0.0 200.8 jit_solution(9745291499909439044)
XLA Ops:
  0.7 0.7 multiply_bitcast_fusion
  1.3 0.1 iota_add_fusion
  1.4 0.1 tile.12
  1.5 0.1 add.108
  1.6 0.6 pad_maximum_fusion.refs_2_
  2.2 0.8 convert_dynamic-update-slice_fusion
  3.0 0.0 copy-start.15
  3.0 0.6 copy-done.15
  3.6 0.0 copy-start
  3.6 183.0 %layer.1 = (bf16[128,1024]{1,0:T(8,128)(2,1)}, bf16[128,1024]{1,0:T(8,128)(2,1)}, bf16[64,4096]{1,0:T(8,128)(2,1)}, bf16[128,1024]{1,0:T(8,128)(2,1)}, bf16[64,6...) custom-call(bf16[128,1024]{1,0:T(8,128)(2,1)} %bitcast.14, bf16[128,1024]{1,0:T(8,128)(2,1)} %bitcast.15, ...), custom_call_target="tpu_custom_call" | custom-call | tf_op jit(solution)/shard_map/layer/pallas_call | solution.py:938
  186.6 0.0 copy-done
  186.6 0.0 copy-start.1
  186.6 0.0 copy-start.4
  186.6 0.0 copy-start.5
  186.6 0.0 copy-start.10
  186.6 5.2 %multiply_subtract_fusion = (f32[64,6144]{1,0:T(8,128)}, f32[64,6144]{1,0:T(8,128)}, f32[64,6144]{1,0:T(8,128)}) fusion(f32[64,6144]{1,0:T(8,128)S(1)} %copy-done, bf16[64,6144]{1,0:T(8,128)(2,1)} %get-tuple-element.28, f32[64,6144]{1,0:T(8,128)} %param.29, f32[64,6144]{1,0:T(8,128)} %param.34), kind=kLoop, calls=%fused_computation.4 | loop fusion | flops 6291456 | bytes 10223616 | tf_op jit(solution)/shard_map/sub | solution.py:958
  191.8 0.0 copy-done.1
  191.8 0.0 copy-done.4
  191.8 0.0 copy-done.5
  191.9 0.0 copy-done.10
  191.9 0.0 copy-start.2
  191.9 0.0 copy-start.6
  191.9 0.0 copy-start.7
  191.9 0.0 copy-start.11
  191.9 2.2 %multiply_subtract_fusion.1 = (f32[64,4096]{1,0:T(8,128)}, f32[64,4096]{1,0:T(8,128)}, f32[64,4096]{1,0:T(8,128)}) fusion(f32[64,4096]{1,0:T(8,128)S(1)} %copy-done.1, bf16[64,4096]{1,0:T(8,128)(2,1)S(1)} %copy-done.10, f32[64,4096]{1,0:T(8,128)S(1)} %copy-done.4, f32[64,4096]{1,0:T(8,128)S(1)} %copy-done.5), kind=kLoop, calls=%fused_computation.10 | loop fusion | flops 4194304 | bytes 6815744 | tf_op jit(solution)/shard_map/sub | solution.py:958
  194.1 0.0 copy-done.2
  194.1 0.0 copy-done.6
  194.1 0.0 copy-done.7
  194.2 0.4 copy-done.11
  194.6 0.0 copy-start.3
  194.6 0.0 copy-start.8
  194.6 0.0 copy-start.9
  194.6 0.0 copy-start.14
  194.6 1.8 multiply_subtract_fusion.2
  196.4 0.0 copy-done.3
  196.4 0.0 copy-done.8
  196.4 0.0 copy-done.9
  196.4 0.1 copy-done.14
  196.6 0.0 copy-start.12
  196.6 1.4 multiply_subtract_fusion.3
  198.0 0.0 copy-done.16
  198.0 0.0 copy-done.17
  198.0 0.0 copy-done.18
  198.0 1.4 multiply_subtract_fusion.4
  199.4 0.0 copy-done.13
  199.4 0.7 copy.41
  200.1 0.0 copy-done.12
  200.1 0.7 copy.42
  (10 shorter events, 0.0 us)
Async XLA Ops:
  3.0 0.6 copy-start.15
  3.6 183.0 %copy-start = (f32[64,6144]{1,0:T(8,128)S(1)}, f32[64,6144]{1,0:T(8,128)}, u32[]{:S(2)}) copy-start(f32[64,6144]{1,0:T(8,128)} %refs_7_.1) | copy-start | bytes 4718596
  186.6 5.3 %copy-start.1 = (f32[64,4096]{1,0:T(8,128)S(1)}, f32[64,4096]{1,0:T(8,128)}, u32[]{:S(2)}) copy-start(f32[64,4096]{1,0:T(8,128)} %refs_5_.1) | copy-start | bytes 3145732
  186.6 5.3 %copy-start.4 = (f32[64,4096]{1,0:T(8,128)S(1)}, f32[64,4096]{1,0:T(8,128)}, u32[]{:S(2)}) copy-start(f32[64,4096]{1,0:T(8,128)} %param.27) | copy-start | bytes 3145732
  186.6 5.3 %copy-start.5 = (f32[64,4096]{1,0:T(8,128)S(1)}, f32[64,4096]{1,0:T(8,128)}, u32[]{:S(2)}) copy-start(f32[64,4096]{1,0:T(8,128)} %param.32) | copy-start | bytes 3145732
  186.6 5.2 %copy-start.10 = (bf16[64,4096]{1,0:T(8,128)(2,1)S(1)}, bf16[64,4096]{1,0:T(8,128)(2,1)}, u32[]{:S(2)}) copy-start(bf16[64,4096]{1,0:T(8,128)(2,1)} %get-tuple-element.26) | copy-start | bytes 1572868
  191.9 2.3 %copy-start.2 = (f32[192,1024]{1,0:T(8,128)S(1)}, f32[192,1024]{1,0:T(8,128)}, u32[]{:S(2)}) copy-start(f32[192,1024]{1,0:T(8,128)} %refs_8_.1) | copy-start | bytes 2359300
  191.9 2.3 %copy-start.6 = (f32[192,1024]{1,0:T(8,128)S(1)}, f32[192,1024]{1,0:T(8,128)}, u32[]{:S(2)}) copy-start(f32[192,1024]{1,0:T(8,128)} %param.30) | copy-start | bytes 2359300
  191.9 2.3 %copy-start.7 = (f32[192,1024]{1,0:T(8,128)S(1)}, f32[192,1024]{1,0:T(8,128)}, u32[]{:S(2)}) copy-start(f32[192,1024]{1,0:T(8,128)} %param.35) | copy-start | bytes 2359300
  191.9 2.7 %copy-start.11 = (bf16[192,1024]{1,0:T(8,128)(2,1)S(1)}, bf16[192,1024]{1,0:T(8,128)(2,1)}, u32[]{:S(2)}) copy-start(bf16[192,1024]{1,0:T(8,128)(2,1)} %get-tuple-element.29) | copy-start | bytes 1179652
  194.6 1.8 copy-start.3
  194.6 1.8 copy-start.8
  194.6 1.8 copy-start.9
  194.6 2.0 copy-start.14
  196.6 1.4 copy-start.16
  196.6 1.4 copy-start.17
  196.6 1.4 copy-start.18
  196.6 2.8 %copy-start.13 = (bf16[128,1024]{1,0:T(8,128)(2,1)S(1)}, bf16[128,1024]{1,0:T(8,128)(2,1)}, u32[]{:S(2)}) copy-start(bf16[128,1024]{1,0:T(8,128)(2,1)} %get-tuple-element.24) | copy-start | bytes 786436
  196.6 3.5 %copy-start.12 = (bf16[128,1024]{1,0:T(8,128)(2,1)S(1)}, bf16[128,1024]{1,0:T(8,128)(2,1)}, u32[]{:S(2)}) copy-start(bf16[128,1024]{1,0:T(8,128)(2,1)} %get-tuple-element.25) | copy-start | bytes 786436
where the time goes:
time: 203 us; the launch traced here: 201 us
  Pallas kernels  183 us (90%)
  other arithmetic  14.2 us (7%)
  local copies, waits for them, and re-layouts  2.85 us (1%)
    pallas_call x1, Pallas kernels, layer(): pl.pallas_call(layer_kernel, out_shape=[jax.ShapeDtypeStruct(shape, kind)...  183 us
    sub x5, other arithmetic, adam_update(): return (weight - rate * (step + decay * weight), moment_new, square_new)  12.1 us

commit v1 on v0

--- a/solution.py
+++ b/solution.py
@@ -85,16 +85,26 @@
     ggu=((D, 768), bf16),
     go=((256, D), bf16),
     gd=((384, D), bf16),
-    rqa=((16, 64, 256), bf16),
-    rqb=((16, 64, 256), bf16),
-    rgu=((16, 64, 768), bf16),
-    ro=((16, 32, 512), bf16),
-    rd=((16, 48, 512), bf16),
-    sqa=((64, 256), bf16),
-    sqb=((64, 256), bf16),
-    sgu=((64, 768), bf16),
-    so=((32, 512), bf16),
-    sd=((48, 512), bf16),
+    zqa=((3, 2, 128, 256), bf16),
+    zqb=((3, 2, 128, 256), bf16),
+    zgu=((3, 2, 128, 768), bf16),
+    zo=((3, 2, 32, D), bf16),
+    zd=((3, 2, 48, D), bf16),
+    sqa=((2, 128, 256), bf16),
+    sqb=((2, 128, 256), bf16),
+    sgu=((2, 128, 768), bf16),
+    so=((2, 32, D), bf16),
+    sd=((2, 48, D), bf16),
+    xqa=((3, 64, 256), bf16),
+    xqb=((3, 64, 256), bf16),
+    xgu=((3, 64, 768), bf16),
+    xo=((3, 32, 512), bf16),
+    xd=((3, 48, 512), bf16),
+    hqa=((2, 64, 256), bf16),
+    hqb=((2, 64, 256), bf16),
+    hgu=((2, 64, 768), bf16),
+    ho=((32, D), bf16),
+    hd=((48, D), bf16),
     fqa=((8, 64, 256), bf16),
     fqb=((8, 64, 256), bf16),
     fgu=((8, 64, 768), bf16),
@@ -102,15 +112,15 @@
     fd=((192, D), bf16),
     dg=((24, 128), f32),
     dg_r1=((8, 24, 128), f32),
-    dg_s=((24, 128), f32),
-    dg_r2=((16, 24, 128), f32),
+    dg_s=((2, 24, 128), f32),
+    dg_r2=((6, 24, 128), f32),
 )
 SEMAPHORES = dict(
     ld=16,
-    s_x=7, r_x=7,
-    s_dy=7, r_dy=7,
-    s_n2=14, r_n2=14,
-    s_dob=14, r_dob=14,
+    s_x=8, r_x=8,
+    s_dy=8, r_dy=8,
+    s_n2=16, r_n2=16,
+    s_dob=16, r_dob=16,
     s_pos=1, r_pos=1,
     s_gain=12, r_gain=12,
     s_wq=12, r_wq=12,
@@ -121,18 +131,18 @@
     s_c=32, r_c=32,
     s_r=24, r_r=24,
     s_dkv=2, r_dkv=2,
-    s_gqa=16, r_gqa=16,
-    s_gqb=16, r_gqb=16,
-    s_ggu=16, r_ggu=16,
-    s_go=16, r_go=16,
-    s_gd=16, r_gd=16,
-    s_fqa=8, r_fqa=8,
-    s_fqb=8, r_fqb=8,
-    s_fgu=8, r_fgu=8,
-    s_fo=8, r_fo=8,
-    s_fd=8, r_fd=8,
+    s_gqa=9, r_gqa=9,
+    s_gqb=9, r_gqb=9,
+    s_ggu=9, r_ggu=9,
+    s_go=9, r_go=9,
+    s_gd=9, r_gd=9,
+    s_fqa=9, r_fqa=9,
+    s_fqb=9, r_fqb=9,
+    s_fgu=9, r_fgu=9,
+    s_fo=5, r_fo=5,
+    s_fd=5, r_fd=5,
     s_dg1=8, r_dg1=8,
-    s_dg2=16, r_dg2=16,
+    s_dg2=6, r_dg2=6,
 )
 
 
@@ -210,52 +220,84 @@
     def greet(device):
         pl.semaphore_signal(barrier, inc=1, device_id=device, device_id_type=MESH)
 
-    def greet_groups(i, carry):
-        a, b, d = lax.div(i, 8), lax.rem(lax.div(i, 2), 4), lax.rem(i, 2)
-        core = lax.rem(k + d, 2)
-        greet(place(lax.rem(xh + a, 2), xl, around(y, b), z, core))
-        greet(place(xh, lax.rem(xl + a, 2), y, around(z, b), core))
-        x_ = lax.rem(x + lax.div(i, 4), 4)
-        greet(place(lax.div(x_, 2), lax.rem(x_, 2), y, around(z, lax.rem(i, 4)), k))
+    def greet_plane(i, carry):
+        greet(place(xh, lax.rem(xl + lax.div(i, 8), 2), y, around(z, lax.rem(lax.div(i, 2), 4)), lax.rem(k + i, 2)))
         return carry
 
     home = (xl == lax.div(t, 4)) & (z == lax.rem(t, 4)) & (k == xl)
 
     def greet_senders(i, carry):
-        @pl.when(jnp.logical_not(home & (lax.div(i, 4) == xh) & (lax.rem(i, 4) == z)))
+        @pl.when(jnp.logical_not(home & (i == z)))
         def _():
-            greet(place(lax.div(i, 4), k, lax.div(part, 2), lax.rem(i, 4), lax.rem(part, 2)))
+            greet(place(xh, k, lax.div(part, 2), i, lax.rem(part, 2)))
 
         return carry
 
-    lax.fori_loop(1, 16, greet_groups, 0)
-    lax.fori_loop(0, 8, greet_senders, 0)
-    pl.semaphore_wait(barrier, 53 - home.astype(jnp.int32))
+    def along_x(d):
+        x_ = around(x, d)
+        return place(lax.div(x_, 2), lax.rem(x_, 2), y, z, k)
+
+    for i in range(1, 8):
+        greet(place(xh, xl, around(y, i // 2), z, lax.rem(k + i, 2)))
+    lax.fori_loop(1, 16, greet_plane, 0)
+    for d in range(1, 4):
+        greet(along_x(d))
+    lax.fori_loop(0, 4, greet_senders, 0)
+
+    for one in loads:
+        one.wait()
+    r.wq_send[...] = r.wq_f[...].astype(bf16)
+    r.wgu_send[...] = r.wgu_fs[...].astype(bf16)
+    r.wo_own[...] = r.wo_f[...].astype(bf16)
+    r.wd_own[...] = r.wd_f[...].astype(bf16)
+    r.wq[f] = r.wq_send[k]
+    r.wgu[f] = r.wgu_send[k]
+    r.gain_recv[f] = r.gain_in[...]
+    r.x_all[y, k] = r.tok[...]
+    r.dy_all[y, k] = r.dyt[...]
+    r.pos[k] = r.pos_in[...]
+    r.dg[...] = jnp.zeros((24, 128), f32)
+    pl.semaphore_wait(barrier, 29 - home.astype(jnp.int32))
 
     def rows_of(half):
         return pl.ds(0, 128) if half is None else pl.ds(64 * half, 64)
 
+    def far_part(half, which):
+        size = 64 if half is None else 32
+        return pl.ds((0 if half is None else 64 * half) + size * which, size)
+
     def gather_start(src, whole, ss, rs, half=None):
-        rows, o = rows_of(half), 7 * (half or 0)
-        for d in (1, 3, 2):
+        rows, o = rows_of(half), 8 * (half or 0)
+        for d in (1, 3):
             send(src.at[rows], whole.at[y, k, rows], ss.at[o + d - 1], rs.at[o + d - 1], place(xh, xl, around(y, d), z, k))
         send(src.at[rows], whole.at[y, k, rows], ss.at[o + 3], rs.at[o + 3], partner)
 
     def gather_forward(whole, ss, rs, d, half=None):
-        rows, o = rows_of(half), 7 * (half or 0)
+        rows, o = rows_of(half), 8 * (half or 0)
         block = whole.at[around(y, 4 - d), k, rows]
-        got(block, rs.at[o + d - 1])
+        if d == 2:
+            for which in range(2):
+                got(whole.at[around(y, 2), k, far_part(half, which)], rs.at[o + (1, 7)[which]])
+        else:
+            got(block, rs.at[o + d - 1])
+            which = 0 if d == 1 else 1
+            part_of = whole.at[around(y, 4 - d), k, far_part(half, which)]
+            i = o + (1, 7)[which]
+            send(part_of, part_of, ss.at[i], rs.at[i], place(xh, xl, around(y, d), z, k))
         send(block, block, ss.at[o + 3 + d], rs.at[o + 3 + d], partner)
 
     def gather_own(whole, rs, half=None):
-        got(whole.at[y, other, rows_of(half)], rs.at[7 * (half or 0) + 3])
+        got(whole.at[y, other, rows_of(half)], rs.at[8 * (half or 0) + 3])
 
     def gather_pair(whole, rs, d, half=None):
-        got(whole.at[around(y, 4 - d), other, rows_of(half)], rs.at[7 * (half or 0) + 3 + d])
+        got(whole.at[around(y, 4 - d), other, rows_of(half)], rs.at[8 * (half or 0) + 3 + d])
 
     def gather_end(whole, ss, half=None):
-        for i in range(7):
-            sent(whole.at[y, k, rows_of(half)], ss.at[7 * (half or 0) + i])
+        o = 8 * (half or 0)
+        for i in (0, 2, 3, 4, 5, 6):
+            sent(whole.at[y, k, rows_of(half)], ss.at[o + i])
+        for i in (1, 7):
+            sent(whole.at[y, k, far_part(half, 0)], ss.at[o + i])
 
     def chip_slots(whole, l_, zz):
         return whole.at[pl.ds(8 * l_ + 2 * zz, 2)]
@@ -271,8 +313,7 @@
                 got(whole.at[8 * xl + 2 * around(z, 4 - dz) + lax.rem(k + dk, 2)], rs.at[2 * dz + dk])
 
     def beside(dz):
-        x_ = around(x, 1 if dz < 2 else 3)
-        return place(lax.div(x_, 2), lax.rem(x_, 2), y, z, k)
+        return along_x(1 if dz < 2 else 3)
 
     def x_send(whole, ss, rs, dz):
         block = chip_slots(whole, xl, around(z, 4 - dz))
@@ -295,17 +336,10 @@
         lax.fori_loop(first, last, one, 0)
 
     gather_start(r.tok, r.x_all, r.s_x, r.r_x)
+    z_send(lambda k_: r.wq_send.at[k_], r.wq, r.s_wq, r.r_wq)
     send(r.pos_in, r.pos.at[k], r.s_pos.at[0], r.r_pos.at[0], partner)
-    for one in loads[:6]:
-        one.wait()
-    r.wq_send[...] = r.wq_f[...].astype(bf16)
-    z_send(lambda k_: r.wq_send.at[k_], r.wq, r.s_wq, r.r_wq)
     z_send(lambda k_: r.gain_in, r.gain_recv, r.s_gain, r.r_gain)
-    r.wq[f] = r.wq_send[k]
-    r.gain_recv[f] = r.gain_in[...]
-
-    r.wo_own[...] = r.wo_f[...].astype(bf16)
-    r.wd_own[...] = r.wd_f[...].astype(bf16)
+
     is_source = lax.div(part, 2) == y
     to_core = lax.rem(part, 2)
     for i in range(4):
@@ -329,13 +363,8 @@
     def wd_rows(q):
         return r.wd.at[pl.ds(pl.multiple_of(48 * q, 16), 48)]
 
-    r.x_all[y, k] = r.tok[...]
-    r.dy_all[y, k] = r.dyt[...]
-    r.pos[k] = r.pos_in[...]
-    for one in loads[6:]:
-        one.wait()
-    r.wgu_send[...] = r.wgu_fs[...].astype(bf16)
-    r.wgu[f] = r.wgu_send[k]
+    z_got(r.wq, r.r_wq, 0)
+    x_send(r.wq, r.s_wq, r.r_wq, 0)
 
     got(r.pos.at[other], r.r_pos.at[0])
     steps = lax.broadcasted_iota(jnp.int32, (BLOCK, 1), 0).astype(f32)
@@ -353,13 +382,19 @@
             r.sin_t[yy, s * 128 : (s + 1) * 128, :] = jnp.sin(angle) * sign
         return carry
 
-    lax.fori_loop(0, 4, tables, 0)
-
-    for dz in (0, 1, 3, 2):
+    lax.fori_loop(0, 2, tables, 0)
+
+    for dz in (1, 3):
+        z_got(r.wq, r.r_wq, dz)
+        x_send(r.wq, r.s_wq, r.r_wq, dz)
+    for d in (1, 3):
+        gather_forward(r.x_all, r.s_x, r.r_x, d)
+    lax.fori_loop(2, 4, tables, 0)
+    z_got(r.wq, r.r_wq, 2)
+    x_send(r.wq, r.s_wq, r.r_wq, 2)
+    for dz in range(4):
         z_got(r.gain_recv, r.r_gain, dz)
         x_send(r.gain_recv, r.s_gain, r.r_gain, dz)
-        z_got(r.wq, r.r_wq, dz)
-        x_send(r.wq, r.s_wq, r.r_wq, dz)
     z_send(lambda k_: r.wgu_send.at[k_], r.wgu, r.s_wgu, r.r_wgu)
     gather_start(r.dyt, r.dy_all, r.s_dy, r.r_dy)
     own_piece = (2 * y + k == part) & (xl == k)
@@ -424,8 +459,6 @@
                     r.q_s[s, half, pl.ds(pl.multiple_of(64 * yy, 64), 64), h * HEAD : (h + 1) * HEAD] = u[first : first + 64]
 
     gather_own(r.x_all, r.r_x)
-    for d in (1, 3):
-        gather_forward(r.x_all, r.s_x, r.r_x, d)
     for dz in range(4):
         x_got(r.wq, r.r_wq, dz)
     project(0)
@@ -567,53 +600,67 @@
         for d in ds:
             reduce_first(1, r.pb, r.cb, d, half)
 
+    def near_forward(whole, ss, rs, half):
+        for d in (1, 3):
+            gather_forward(whole, ss, rs, d, half)
+
+    near_forward(r.n2_all, r.s_n2, r.r_n2, 0)
     for half in range(2):
         gather_own(r.n2_all, r.r_n2, half)
-        for d in (1, 3):
-            gather_forward(r.n2_all, r.s_n2, r.r_n2, d, half)
         gather_pair(r.n2_all, r.r_n2, 1, half)
         feed((0, 3), half)
         gather_forward(r.n2_all, r.s_n2, r.r_n2, 2, half)
+        if half == 0:
+            near_forward(r.n2_all, r.s_n2, r.r_n2, 1)
         gather_pair(r.n2_all, r.r_n2, 3, half)
         gather_pair(r.n2_all, r.r_n2, 2, half)
         feed((2, 1), half)
         for d in (3, 2, 1):
             reduce_second(1, r.pb, r.cb, r.rb, d, half)
 
-    def cross(i, sign):
-        dx, dz = lax.div(i, 4), lax.rem(i, 4)
-        x_, z_ = lax.rem(x + 4 + sign * dx, 4), lax.rem(z + 4 + sign * dz, 4)
-        return lax.div(x_, 2), lax.rem(x_, 2), z_
-
-    def cross_send(piece_of, dst, ss, rs):
-        def one(i, carry):
-            h_, l_, z_ = cross(i, 1)
-            send(piece_of(h_, 4 * l_ + z_), dst.at[i], ss.at[i], rs.at[i], place(h_, l_, y, z_, k))
-            return carry
-
-        lax.fori_loop(1, 16, one, 0)
-
-    def cross_sum(own, dst, rs):
-        def one(i, total):
-            got(dst.at[i], rs.at[i])
-            return total + dst[i].astype(f32)
-
-        return lax.fori_loop(1, 16, one, own.astype(f32))
-
-    def piece_rows(whole, height):
-        def of(h_, p_):
-            return whole.at[pl.ds(pl.multiple_of(2 * height * p_ + height * h_, height), height)]
-
-        return of
-
-    def piece_block(whole, height):
-        def of(h_, p_):
-            return whole.at[pl.ds(pl.multiple_of(height * p_, 16), height), pl.ds(pl.multiple_of(512 * h_, 512), 512)]
-
-        return of
-
-    gqa_piece, gqb_piece, ggu_piece = piece_rows(r.gqa, 64), piece_rows(r.gqb, 64), piece_rows(r.ggu, 64)
-    go_piece, gd_piece = piece_block(r.go, 32), piece_block(r.gd, 48)
+    def rows_at(whole, height):
+        return lambda l_, z_: whole.at[pl.ds(pl.multiple_of(height * (4 * l_ + z_), 16), height)]
+
+    def cross_z(piece, dst, ss, rs):
+        for dz in (1, 3, 2):
+            zz = around(z, dz)
+            for l_ in range(2):
+                i = 2 * (dz - 1) + l_
+                send(piece(l_, zz), dst.at[dz - 1, l_], ss.at[i], rs.at[i], place(xh, xl, y, zz, k))
+
+    def row_half(ref, h_):
+        return ref.at[pl.ds(pl.multiple_of(64 * h_, 64), 64)]
+
+    def column_half(ref, h_):
+        return ref.at[:, pl.ds(pl.multiple_of(512 * h_, 512), 512)]
+
+    def cross_x(piece, zrecv, sums, xrecv, half_of, ss, rs):
+        for l_ in range(2):
+            total = piece(l_, z)[...].astype(f32)
+            for dz in range(1, 4):
+                got(zrecv.at[dz - 1, l_], rs.at[2 * (dz - 1) + l_])
+                total = total + zrecv[dz - 1, l_].astype(f32)
+            sums[l_] = total.astype(bf16)
+        for dx in (1, 3, 2):
+            x_ = around(x, dx)
+            block = half_of(sums.at[lax.rem(x_, 2)], lax.div(x_, 2))
+            send(block, xrecv.at[dx - 1], ss.at[5 + dx], rs.at[5 + dx], along_x(dx))
+
+    def cross_total(sums, xrecv, half_of, rs):
+        total = half_of(sums.at[xl], xh)[...].astype(f32)
+        for dx in (1, 3, 2):
+            got(xrecv.at[dx - 1], rs.at[5 + dx])
+            total = total + xrecv[dx - 1].astype(f32)
+        return total
+
+    def cross_sent(zrecv, xrecv, ss):
+        for i in range(6):
+            sent(zrecv.at[0, 0], ss.at[i])
+        for i in range(3):
+            sent(xrecv.at[0], ss.at[6 + i])
+
+    gqa_piece, gqb_piece, ggu_piece = rows_at(r.gqa, 128), rows_at(r.gqb, 128), rows_at(r.ggu, 128)
+    go_piece, gd_piece = rows_at(r.go, 32), rows_at(r.gd, 48)
 
     def weight_gradient(left, right, out):
         def one(i, carry):
@@ -622,8 +669,6 @@
             return carry
 
         lax.fori_loop(0, out.shape[1] // 256, one, 0)
-
-    r.dg[...] = jnp.zeros((24, 128), f32)
 
     def middle_back(half):
         rows = rows_of(half)
@@ -645,7 +690,7 @@
         lambda cols: r.dy_all[:, :, :, cols].reshape(D, 256),
         r.gd,
     )
-    cross_send(gd_piece, r.rd, r.s_gd, r.r_gd)
+    cross_z(gd_piece, r.zd, r.s_gd, r.r_gd)
     middle_back(0)
     weight_gradient(
         lambda: r.n2_all[...].reshape(D, D),
@@ -653,7 +698,7 @@
         r.ggu,
     )
     middle_back(1)
-    cross_send(ggu_piece, r.rgu, r.s_ggu, r.r_ggu)
+    cross_z(ggu_piece, r.zgu, r.s_ggu, r.r_ggu)
 
     def norm_back(value, gain, grad):
         inverse = inverse_rms(value)
@@ -694,9 +739,8 @@
             r.dg[16:17, :] += gain_grad
 
     def gather_rest(half):
+        gather_forward(r.x_all, r.s_dob, r.r_dob, 2, half)
         gather_own(r.x_all, r.r_dob, half)
-        for d in (1, 3, 2):
-            gather_forward(r.x_all, r.s_dob, r.r_dob, d, half)
         for d in (1, 3, 2):
             gather_pair(r.x_all, r.r_dob, d, half)
 
@@ -711,12 +755,15 @@
     lax.fori_loop(0, 4, down_partial, 0)
     for d in (2, 1, 3, 0):
         reduce_first(2, r.pa, r.ca, d)
+    near_forward(r.x_all, r.s_dob, r.r_dob, 0)
     gather_rest(0)
-    for s in range(2):
-        attend_back(0, s)
+    attend_back(0, 0)
+    near_forward(r.x_all, r.s_dob, r.r_dob, 1)
+    attend_back(0, 1)
     gather_rest(1)
     for d in (2, 1, 3):
         reduce_second(2, r.pa, r.ca, r.ra, d)
+    cross_x(gd_piece, r.zd, r.sd, r.xd, column_half, r.s_gd, r.r_gd)
     for s in range(2):
         attend_back(1, s)
         r.dkv_send[s] = r.dkv[s, pl.ds(pl.multiple_of(512 * (1 - xh), 512), 512), :].astype(bf16)
@@ -729,7 +776,7 @@
         return prod[:, 0:128] + prod[:, 128:256]
 
     r.wdot[...] = qkv_gradient(0, r.gqa)
-    cross_send(gqa_piece, r.rqa, r.s_gqa, r.r_gqa)
+    cross_z(gqa_piece, r.zqa, r.s_gqa, r.r_gqa)
 
     def out_gradient(i, carry):
         cols = pl.ds(pl.multiple_of(256 * i, 256), 256)
@@ -742,39 +789,44 @@
         return carry
 
     lax.fori_loop(0, 4, out_gradient, 0)
-    cross_send(go_piece, r.ro, r.s_go, r.r_go)
-
-    def spread_rows(total, hold, final, ss, rs):
-        hold[...] = total.astype(bf16)
-
+    cross_z(go_piece, r.zo, r.s_go, r.r_go)
+
+    other_half = place(1 - xh, xl, y, z, k)
+
+    def rows_exchange(total, hold, ss, rs):
+        hold[xh] = total.astype(bf16)
+        send(hold.at[xh], hold.at[xh], ss.at[8], rs.at[8], other_half)
+
+    def rows_spread(hold, final, ss, rs):
+        for which in range(2):
+            h = xh if which == 0 else 1 - xh
+            if which == 1:
+                got(hold.at[h], rs.at[8])
+            for i in (2, 1, 3):
+                send(hold.at[h], final.at[t], ss.at[4 * which + i], rs.at[t], place(xh, xl, around(y, i), z, h))
+
+            @pl.when(k != h)
+            def _():
+                send(hold.at[h], final.at[t], ss.at[4 * which], rs.at[t], partner)
+
+            @pl.when(k == h)
+            def _():
+                final[t] = hold[h]
+
+    def rows_spread_sent(hold, ss):
+        sent(hold.at[0], ss.at[8])
+        for which in range(2):
+            h = xh if which == 0 else 1 - xh
+            for i in range(1, 4):
+                sent(hold.at[0], ss.at[4 * which + i])
+
+            @pl.when(k != h)
+            def _():
+                sent(hold.at[0], ss.at[4 * which])
+
+    def rows_spread_got(final, rs):
         def one(i, carry):
-            there = place(lax.rem(xh + lax.div(i, 4), 2), xl, lax.rem(y + i, 4), z, xh)
-
-            @pl.when((i > 0) | (k != xh))
-            def _():
-                send(hold, final.at[t], ss.at[i], rs.at[t], there)
-
-            return carry
-
-        lax.fori_loop(0, 8, one, 0)
-
-        @pl.when(k == xh)
-        def _():
-            final[t] = hold[...]
-
-    def spread_rows_sent(hold, ss):
-        def one(i, carry):
-            @pl.when((i > 0) | (k != xh))
-            def _():
-                sent(hold, ss.at[i])
-
-            return carry
-
-        lax.fori_loop(0, 8, one, 0)
-
-    def spread_rows_got(final, rs):
-        def one(i, carry):
-            @pl.when((i != t) | (k != xh))
+            @pl.when(i != t)
             def _():
                 got(final.at[i], rs.at[i])
 
@@ -782,50 +834,57 @@
 
         lax.fori_loop(0, 8, one, 0)
 
-    def spread_block(total, hold, final, height, ss, rs):
-        hold[...] = total.astype(bf16)
+    def block_exchange(total, hold, ss, rs):
+        column_half(hold, xh)[...] = total.astype(bf16)
+        send(column_half(hold, xh), column_half(hold, xh), ss.at[4], rs.at[4], other_half)
+
+    def block_spread(hold, final, height, ss, rs):
+        got(column_half(hold, 1 - xh), rs.at[4])
         rows = pl.ds(pl.multiple_of(height * z, 16), height)
-        cols = pl.ds(pl.multiple_of(512 * xh, 512), 512)
-
-        def one(i, carry):
-            there = place(lax.rem(xh + lax.div(i, 4), 2), lax.div(t, 4), lax.rem(y + i, 4), lax.rem(t, 4), xl)
-
-            @pl.when((i > 0) | jnp.logical_not(home))
-            def _():
-                send(hold, final.at[rows, cols], ss.at[i], rs.at[4 * xh + z], there)
-
-            return carry
-
-        lax.fori_loop(0, 8, one, 0)
+
+        def to(i):
+            there = place(xh, lax.div(t, 4), around(y, i), lax.rem(t, 4), xl)
+            send(hold, final.at[rows], ss.at[i], rs.at[z], there)
+
+        for i in (2, 1, 3):
+            to(i)
+
+        @pl.when(jnp.logical_not(home))
+        def _():
+            to(0)
 
         @pl.when(home)
         def _():
-            final[rows, cols] = hold[...]
-
-    def spread_block_sent(hold, ss):
+            final[rows, :] = hold[...]
+
+    def block_spread_sent(hold, ss):
+        sent(column_half(hold, 0), ss.at[4])
+        for i in range(1, 4):
+            sent(hold, ss.at[i])
+
+        @pl.when(jnp.logical_not(home))
+        def _():
+            sent(hold, ss.at[0])
+
+    def block_spread_got(final, height, rs):
         def one(i, carry):
-            @pl.when((i > 0) | jnp.logical_not(home))
+            @pl.when((i != z) | jnp.logical_not(home))
             def _():
-                sent(hold, ss.at[i])
+                got(final.at[pl.ds(pl.multiple_of(height * i, 16), height)], rs.at[i])
 
             return carry
 
-        lax.fori_loop(0, 8, one, 0)
-
-    def spread_block_got(final, height, rs):
-        def one(i, carry):
-            @pl.when((i != 4 * xh + z) | jnp.logical_not(home))
-            def _():
-                rows = pl.ds(pl.multiple_of(height * lax.rem(i, 4), 16), height)
-                cols = pl.ds(pl.multiple_of(512 * lax.div(i, 4), 512), 512)
-                got(final.at[rows, cols], rs.at[i])
-
-            return carry
-
-        lax.fori_loop(0, 8, one, 0)
-
-    spread_block(cross_sum(gd_piece(xh, part)[...], r.rd, r.r_gd), r.sd, r.fd, 48, r.s_fd, r.r_fd)
-    spread_rows(cross_sum(ggu_piece(xh, part)[...], r.rgu, r.r_ggu), r.sgu, r.fgu, r.s_fgu, r.r_fgu)
+        lax.fori_loop(0, 4, one, 0)
+
+    cross_x(ggu_piece, r.zgu, r.sgu, r.xgu, row_half, r.s_ggu, r.r_ggu)
+    block_exchange(cross_total(r.sd, r.xd, column_half, r.r_gd), r.hd, r.s_fd, r.r_fd)
+    rows_exchange(cross_total(r.sgu, r.xgu, row_half, r.r_ggu), r.hgu, r.s_fgu, r.r_fgu)
+    block_spread(r.hd, r.fd, 48, r.s_fd, r.r_fd)
+    rows_spread(r.hgu, r.fgu, r.s_fgu, r.r_fgu)
+    cross_x(gqa_piece, r.zqa, r.sqa, r.xqa, row_half, r.s_gqa, r.r_gqa)
+    cross_x(go_piece, r.zo, r.so, r.xo, column_half, r.s_go, r.r_go)
+    out_tokens = r.h1[...] + reduce_third(2, r.pa, r.ca, r.ra)
+    r.out_tok[...] = out_tokens.astype(bf16)
 
     for half in range(2):
         reduce_end(1, r.pb, half)
@@ -851,7 +910,7 @@
         r.pb[yy] = dn1.astype(bf16).reshape(2, 128, D)
         reduce_first(3, r.pb, r.cb, d)
     wdot = r.wdot[...] + qkv_gradient(256, r.gqb)
-    cross_send(gqb_piece, r.rqb, r.s_gqb, r.r_gqb)
+    cross_z(gqb_piece, r.zqb, r.s_gqb, r.r_gqb)
     for d in (2, 1, 3):
         reduce_second(3, r.pb, r.cb, r.rb, d)
     dg1 = jnp.sum(wdot.T, axis=0, keepdims=True) / g1
@@ -861,36 +920,48 @@
         there = place(xh, xl, around(y, i // 2), z, lax.rem(k + i, 2))
         send(r.dg, r.dg_r1.at[i], r.s_dg1.at[i], r.r_dg1.at[i], there)
 
-    spread_rows(cross_sum(gqa_piece(xh, part)[...], r.rqa, r.r_gqa), r.sqa, r.fqa, r.s_fqa, r.r_fqa)
-    spread_block(cross_sum(go_piece(xh, part)[...], r.ro, r.r_go), r.so, r.fo, 32, r.s_fo, r.r_fo)
-    out_tokens = r.h1[...] + reduce_third(2, r.pa, r.ca, r.ra)
-    r.out_tok[...] = out_tokens.astype(bf16)
+    rows_exchange(cross_total(r.sqa, r.xqa, row_half, r.r_gqa), r.hqa, r.s_fqa, r.r_fqa)
+    block_exchange(cross_total(r.so, r.xo, column_half, r.r_go), r.ho, r.s_fo, r.r_fo)
     total = r.dg[...]
     for i in range(1, 8):
         got(r.dg_r1.at[i], r.r_dg1.at[i])
         total = total + r.dg_r1[i]
-    r.dg_s[...] = total
-    cross_send(lambda h_, p_: r.dg_s, r.dg_r2, r.s_dg2, r.r_dg2)
-    spread_rows(cross_sum(gqb_piece(xh, part)[...], r.rqb, r.r_gqb), r.sqb, r.fqb, r.s_fqb, r.r_fqb)
+    r.dg_s[0] = total
+    for dz in range(1, 4):
+        send(r.dg_s.at[0], r.dg_r2.at[dz - 1], r.s_dg2.at[dz - 1], r.r_dg2.at[dz - 1], place(xh, xl, y, around(z, dz), k))
+    rows_spread(r.hqa, r.fqa, r.s_fqa, r.r_fqa)
+    block_spread(r.ho, r.fo, 32, r.s_fo, r.r_fo)
+    cross_x(gqb_piece, r.zqb, r.sqb, r.xqb, row_half, r.s_gqb, r.r_gqb)
+    for dz in range(1, 4):
+        got(r.dg_r2.at[dz - 1], r.r_dg2.at[dz - 1])
+        total = total + r.dg_r2[dz - 1]
+    r.dg_s[1] = total
+    for dx in range(1, 4):
+        send(r.dg_s.at[1], r.dg_r2.at[2 + dx], r.s_dg2.at[2 + dx], r.r_dg2.at[2 + dx], along_x(dx))
+    rows_exchange(cross_total(r.sqb, r.xqb, row_half, r.r_gqb), r.hqb, r.s_fqb, r.r_fqb)
 
     dn1 = reduce_third(3, r.pb, r.cb, r.rb)
     rows = r.tok[...].astype(f32)
     back, unused = norm_back(rows, g1, dn1)
     r.dtok[...] = (r.dh1[...] + back).astype(bf16)
-
-    spread_block_got(r.fd, 48, r.r_fd)
+    rows_spread(r.hqb, r.fqb, r.s_fqb, r.r_fqb)
+
+    block_spread_got(r.fd, 48, r.r_fd)
     r.g_dn[...] = r.fd[...]
-    spread_rows_got(r.fgu, r.r_fgu)
+    rows_spread_got(r.fgu, r.r_fgu)
     for i in range(8):
         r.g_gu[:, 384 * i : 384 * (i + 1)] = r.fgu[i, :, 0:384]
         r.g_gu[:, 3072 + 384 * i : 3072 + 384 * (i + 1)] = r.fgu[i, :, 384:768]
-    spread_block_got(r.fo, 32, r.r_fo)
+    block_spread_got(r.fo, 32, r.r_fo)
     r.g_out[...] = r.fo[...]
-    spread_rows_got(r.fqa, r.r_fqa)
+    rows_spread_got(r.fqa, r.r_fqa)
     for i in range(8):
         r.g_qkv[:, 256 * i : 256 * (i + 1)] = r.fqa[i]
-    r.g_gain[...] = cross_sum(r.dg_s[...], r.dg_r2, r.r_dg2)
-    spread_rows_got(r.fqb, r.r_fqb)
+    for dx in range(1, 4):
+        got(r.dg_r2.at[2 + dx], r.r_dg2.at[2 + dx])
+        total = total + r.dg_r2[2 + dx]
+    r.g_gain[...] = total
+    rows_spread_got(r.fqb, r.r_fqb)
     for i in range(8):
         r.g_qkv[:, 2048 + 128 * i : 2048 + 128 * (i + 1)] = r.fqb[i, :, 0:128]
         r.g_qkv[:, 3072 + 128 * i : 3072 + 128 * (i + 1)] = r.fqb[i, :, 128:256]
@@ -917,18 +988,17 @@
     reduce_end(3, r.pb)
     for s in range(2):
         sent(r.dkv_send.at[s], r.s_dkv.at[s])
-    loop_sent(gqa_piece(xh, part), r.s_gqa, 1, 16)
-    loop_sent(gqb_piece(xh, part), r.s_gqb, 1, 16)
-    loop_sent(ggu_piece(xh, part), r.s_ggu, 1, 16)
-    loop_sent(go_piece(xh, part), r.s_go, 1, 16)
-    loop_sent(gd_piece(xh, part), r.s_gd, 1, 16)
-    spread_rows_sent(r.sqa, r.s_fqa)
-    spread_rows_sent(r.sqb, r.s_fqb)
-    spread_rows_sent(r.sgu, r.s_fgu)
-    spread_block_sent(r.so, r.s_fo)
-    spread_block_sent(r.sd, r.s_fd)
+    cross_sent(r.zqa, r.xqa, r.s_gqa)
+    cross_sent(r.zqb, r.xqb, r.s_gqb)
+    cross_sent(r.zgu, r.xgu, r.s_ggu)
+    cross_sent(r.zo, r.xo, r.s_go)
+    cross_sent(r.zd, r.xd, r.s_gd)
+    for hold, ss in ((r.hqa, r.s_fqa), (r.hqb, r.s_fqb), (r.hgu, r.s_fgu)):
+        rows_spread_sent(hold, ss)
+    block_spread_sent(r.ho, r.s_fo)
+    block_spread_sent(r.hd, r.s_fd)
     loop_sent(r.dg, r.s_dg1, 1, 8)
-    loop_sent(r.dg_s, r.s_dg2, 1, 16)
+    loop_sent(r.dg_s.at[0], r.s_dg2, 0, 6)
 
 
 def layer(*args):

time: 203 us -> 205 us (level)
  Pallas kernels: 183 us -> 187 us
    pallas_call x1, Pallas kernels: 183 us -> 187 us  [layer(): pl.pallas_call(layer_kernel, out_shape=[jax.ShapeDtypeStruct(shape, kind)...]
where the time goes in v1:
time: 205 us
  Pallas kernels  187 us (91%)
  other arithmetic  14.2 us (7%)
  local copies, waits for them, and re-layouts  2.85 us (1%)
    pallas_call x1, Pallas kernels, layer(): pl.pallas_call(layer_kernel, out_shape=[jax.ShapeDtypeStruct(shape, kind)...  187 us
    sub x5, other arithmetic, adam_update(): return (weight - rate * (step + decay * weight), moment_new, square_new)  12.1 us

profile of v1, /device:TPU:1, one launch (start us, length us, event | category | flops | bytes accessed | tf_op | source)
XLA Modules:
  0.0 204.7 jit_solution(16448932907185410322)
XLA Ops:
  0.7 0.7 multiply_bitcast_fusion
  1.3 0.1 iota_add_fusion
  1.4 0.1 tile.12
  1.5 0.1 add.108
  1.6 0.6 pad_maximum_fusion.refs_2_
  2.2 0.8 convert_dynamic-update-slice_fusion
  3.0 0.0 copy-start.15
  3.0 0.6 copy-done.15
  3.6 186.9 %layer.1 = (bf16[128,1024]{1,0:T(8,128)(2,1)}, bf16[128,1024]{1,0:T(8,128)(2,1)}, bf16[64,4096]{1,0:T(8,128)(2,1)}, bf16[128,1024]{1,0:T(8,128)(2,1)}, bf16[64,6...) custom-call(bf16[128,1024]{1,0:T(8,128)(2,1)} %bitcast.14, bf16[128,1024]{1,0:T(8,128)(2,1)} %bitcast.15, ...), custom_call_target="tpu_custom_call" | custom-call | tf_op jit(solution)/shard_map/layer/pallas_call | solution.py:1008
  190.5 0.0 copy-done
  190.5 0.0 copy-start.1
  190.5 0.0 copy-start.4
  190.5 0.0 copy-start.5
  190.5 0.0 copy-start.10
  190.5 5.2 %multiply_subtract_fusion = (f32[64,6144]{1,0:T(8,128)}, f32[64,6144]{1,0:T(8,128)}, f32[64,6144]{1,0:T(8,128)}) fusion(f32[64,6144]{1,0:T(8,128)S(1)} %copy-done, bf16[64,6144]{1,0:T(8,128)(2,1)} %get-tuple-element.28, f32[64,6144]{1,0:T(8,128)} %param.29, f32[64,6144]{1,0:T(8,128)} %param.34), kind=kLoop, calls=%fused_computation.4 | loop fusion | flops 6291456 | bytes 10223616 | tf_op jit(solution)/shard_map/sub | solution.py:1028
  195.8 0.0 copy-done.1
  195.8 0.0 copy-done.4
  195.8 0.0 copy-done.5
  195.8 0.0 copy-done.10
  195.8 0.0 copy-start.2
  195.8 0.0 copy-start.6
  195.8 0.0 copy-start.7
  195.8 0.0 copy-start.11
  195.8 2.2 %multiply_subtract_fusion.1 = (f32[64,4096]{1,0:T(8,128)}, f32[64,4096]{1,0:T(8,128)}, f32[64,4096]{1,0:T(8,128)}) fusion(f32[64,4096]{1,0:T(8,128)S(1)} %copy-done.1, bf16[64,4096]{1,0:T(8,128)(2,1)S(1)} %copy-done.10, f32[64,4096]{1,0:T(8,128)S(1)} %copy-done.4, f32[64,4096]{1,0:T(8,128)S(1)} %copy-done.5), kind=kLoop, calls=%fused_computation.10 | loop fusion | flops 4194304 | bytes 6815744 | tf_op jit(solution)/shard_map/sub | solution.py:1028
  198.0 0.0 copy-done.2
  198.1 0.0 copy-done.6
  198.1 0.0 copy-done.7
  198.1 0.4 copy-done.11
  198.5 0.0 copy-start.3
  198.5 0.0 copy-start.8
  198.5 0.0 copy-start.9
  198.5 0.0 copy-start.14
  198.5 1.8 multiply_subtract_fusion.2
  200.3 0.0 copy-done.3
  200.3 0.0 copy-done.8
  200.3 0.0 copy-done.9
  200.3 0.1 copy-done.14
  200.5 0.0 copy-start.16
  200.5 0.0 copy-start.12
  200.5 1.4 multiply_subtract_fusion.3
  201.9 0.0 copy-done.16
  201.9 0.0 copy-done.17
  201.9 0.0 copy-done.18
  201.9 1.4 multiply_subtract_fusion.4
  203.3 0.0 copy-done.13
  203.3 0.7 copy.41
  204.0 0.0 copy-done.12
  204.0 0.7 copy.42
  (10 shorter events, 0.0 us)
Async XLA Ops:
  3.0 0.6 copy-start.15
  3.6 186.9 %copy-start = (f32[64,6144]{1,0:T(8,128)S(1)}, f32[64,6144]{1,0:T(8,128)}, u32[]{:S(2)}) copy-start(f32[64,6144]{1,0:T(8,128)} %refs_7_.1) | copy-start | bytes 4718596
  190.5 5.3 %copy-start.1 = (f32[64,4096]{1,0:T(8,128)S(1)}, f32[64,4096]{1,0:T(8,128)}, u32[]{:S(2)}) copy-start(f32[64,4096]{1,0:T(8,128)} %refs_5_.1) | copy-start | bytes 3145732
  190.5 5.3 %copy-start.4 = (f32[64,4096]{1,0:T(8,128)S(1)}, f32[64,4096]{1,0:T(8,128)}, u32[]{:S(2)}) copy-start(f32[64,4096]{1,0:T(8,128)} %param.27) | copy-start | bytes 3145732
  190.5 5.3 %copy-start.5 = (f32[64,4096]{1,0:T(8,128)S(1)}, f32[64,4096]{1,0:T(8,128)}, u32[]{:S(2)}) copy-start(f32[64,4096]{1,0:T(8,128)} %param.32) | copy-start | bytes 3145732
  190.5 5.2 %copy-start.10 = (bf16[64,4096]{1,0:T(8,128)(2,1)S(1)}, bf16[64,4096]{1,0:T(8,128)(2,1)}, u32[]{:S(2)}) copy-start(bf16[64,4096]{1,0:T(8,128)(2,1)} %get-tuple-element.26) | copy-start | bytes 1572868
  195.8 2.3 %copy-start.2 = (f32[192,1024]{1,0:T(8,128)S(1)}, f32[192,1024]{1,0:T(8,128)}, u32[]{:S(2)}) copy-start(f32[192,1024]{1,0:T(8,128)} %refs_8_.1) | copy-start | bytes 2359300
  195.8 2.3 %copy-start.6 = (f32[192,1024]{1,0:T(8,128)S(1)}, f32[192,1024]{1,0:T(8,128)}, u32[]{:S(2)}) copy-start(f32[192,1024]{1,0:T(8,128)} %param.30) | copy-start | bytes 2359300
  195.8 2.3 %copy-start.7 = (f32[192,1024]{1,0:T(8,128)S(1)}, f32[192,1024]{1,0:T(8,128)}, u32[]{:S(2)}) copy-start(f32[192,1024]{1,0:T(8,128)} %param.35) | copy-start | bytes 2359300
  195.8 2.7 %copy-start.11 = (bf16[192,1024]{1,0:T(8,128)(2,1)S(1)}, bf16[192,1024]{1,0:T(8,128)(2,1)}, u32[]{:S(2)}) copy-start(bf16[192,1024]{1,0:T(8,128)(2,1)} %get-tuple-element.29) | copy-start | bytes 1179652
  198.5 1.8 copy-start.3
  198.5 1.8 copy-start.8
  198.5 1.8 copy-start.9
  198.5 2.0 copy-start.14
  200.5 1.4 copy-start.16
  200.5 1.4 copy-start.17
  200.5 1.4 copy-start.18
  200.5 2.8 %copy-start.13 = (bf16[128,1024]{1,0:T(8,128)(2,1)S(1)}, bf16[128,1024]{1,0:T(8,128)(2,1)}, u32[]{:S(2)}) copy-start(bf16[128,1024]{1,0:T(8,128)(2,1)} %get-tuple-element.24) | copy-start | bytes 786436
  200.5 3.5 %copy-start.12 = (bf16[128,1024]{1,0:T(8,128)(2,1)S(1)}, bf16[128,1024]{1,0:T(8,128)(2,1)}, u32[]{:S(2)}) copy-start(bf16[128,1024]{1,0:T(8,128)(2,1)} %get-tuple-element.25) | copy-start | bytes 786436
